TPU v7x, 256 devices: a whole 4x4x8 slice. The times are simulated.
256 devices in a mesh: pieces: 64 (over y, z, core), grp: 4 (over x).
Axes of the slice: x: 4, y: 4, z: 8, core: 2. Of those that a mesh axis runs over, the one named last changes fastest.
Arguments:
- embeddings: bfloat16 [196608, 4096], P(('pieces', 'grp')), may hold values from -6 to 6
- cluster_ids: int32 [196608], P(('pieces', 'grp')), may hold values from 0 to 511, never falling along the last dimension, each value on 1 to 1537 neighbouring positions
Outputs:
- best_match: float32 [196608], P(('pieces', 'grp'))
Inputs may be any that keep to these rules, and one draw needn't show every extreme that they name: `cluster_ids`: never falling along the documents; each cluster holds 1 to 1537 consecutive documents and one holds exactly 1537, so a cluster's documents lie on at most 3 consecutive devices of pieces+grp.
All inputs are finite; a program needn't handle non-finite values.
Results may differ from a plain program's by a relative error of at most 0.0014.
Values may be sent and summed in bfloat16 or wider, within the bound.
A program may use at most 64 MiB of HBM per device.

v0:
```python
import jax
import jax.numpy as jnp
from jax import lax
from jax.sharding import PartitionSpec as P

SPAN = 3


def passed_along(block, axis, distance):
    devices = range(lax.axis_size(axis))
    route = [(i - distance, i) for i in devices if i - distance in devices]
    return lax.ppermute(block, axis, route)


def normalize(rows):
    wide = rows.astype(jnp.float32)
    return (wide * lax.rsqrt(jnp.sum(wide * wide, axis=1, keepdims=True) + 1e-06)).astype(
        jnp.bfloat16
    )


def lifted_tile(own, own_ids, other, other_ids):
    scores = jnp.dot(own, other.T, preferred_element_type=jnp.float32) + 1.0
    keep = own_ids[:, None] == other_ids[None, :]
    lifted = jnp.where(keep, scores, 0.0)
    return (jnp.max(lifted, axis=1), jnp.max(lifted, axis=0))


def shards(embeddings, cluster_ids):
    unit = normalize(embeddings)
    count = unit.shape[0]
    local = jnp.arange(count, dtype=jnp.int32)
    scores = jnp.dot(unit, unit.T, preferred_element_type=jnp.float32) + 1.0
    keep = (cluster_ids[:, None] == cluster_ids[None, :]) & (local[:, None] != local[None, :])
    best = jnp.max(jnp.where(keep, scores, 0.0), axis=1)
    tagged = cluster_ids + 1
    held = (unit, tagged)
    returned = []
    for step in range(1, SPAN):
        held = passed_along((unit, tagged), ("pieces", "grp"), -step)
        other = held[0]
        other_ids = held[1] - 1
        row_part, col_part = lifted_tile(unit, cluster_ids, other, other_ids)
        best = jnp.maximum(best, row_part)
        returned.append(col_part)
    for step in range(1, SPAN):
        best = jnp.maximum(best, passed_along(returned[step - 1], ("pieces", "grp"), step))
    return best - 1.0


def solution(mesh):
    return jax.shard_map(
        shards,
        mesh=mesh,
        in_specs=(P(("pieces", "grp"), None), P(("pieces", "grp"))),
        out_specs=P(("pieces", "grp")),
        check_vma=False,
    )
```

profile of v0, /device:TPU:96, one launch (start us, length us, event | category | flops | bytes accessed | tf_op | source)
XLA Modules:
  0.0 330.2 jit_solution(10908353284771879518)
XLA Ops:
  0.0 0.0 copy-start
  0.0 4.2 %fusion = f32[768]{0:T(1024)S(1)} fusion(bf16[768,4096]{1,0:T(8,128)(2,1)} %param.2), kind=kLoop, calls=%fused_computation.2 | loop fusion | flops 9436416 | bytes 6294528 | tf_op jit(solution)/shard_map/reduce_sum | solution.py:17
  4.2 0.4 copy-done
  4.6 0.0 copy-start.1
  4.6 2.3 fusion.1
  6.9 3.9 %collective-permute-start.3 = (bf16[768,4096]{1,0:T(8,128)(2,1)S(1)}, bf16[768,4096]{1,0:T(8,128)(2,1)S(1)}, u32[]{:S(2)}, u32[]{:S(2)}) collective-permute-start(bf16[768,4096]{1,0:T(8,128)(2,1)S(1)} %fusion.1), channel_id=1, source_target_pairs={{2,0},{3,1},{4,2},{5,3},{6,4},{7,5},{8,6},{9,7},{10,8},{11,9},{12,... | collective-permute-start | bytes 18874376 | tf_op jit(solution)/shard_map/ppermute | solution.py:12
  10.9 2.8 collective-permute-start.1
  13.6 0.0 copy-done.1
  13.7 3.7 %collective-permute-start.2 = (s32[768]{0:T(1024)S(1)}, s32[768]{0:T(1024)S(1)}, u32[]{:S(2)}, u32[]{:S(2)}) collective-permute-start(s32[768]{0:T(1024)S(1)} %broadcast_add_fusion.2), channel_id=1, source_target_pairs={{2,0},{3,1},{4,2},{5,3},{6,4},{7,5},{8,6},{9,7},{10,8},{11,9},{12,... | collective-permute-start | bytes 9224 | tf_op jit(solution)/shard_map/ppermute | solution.py:12
  17.4 3.8 %collective-permute-start = (s32[768]{0:T(1024)S(1)}, s32[768]{0:T(1024)S(1)}, u32[]{:S(2)}, u32[]{:S(2)}) collective-permute-start(s32[768]{0:T(1024)S(1)} %broadcast_add_fusion.2), channel_id=1, source_target_pairs={{1,0},{2,1},{3,2},{4,3},{5,4},{6,5},{7,6},{8,7},{9,8},{10,9},{11,1... | collective-permute-start | bytes 9224 | tf_op jit(solution)/shard_map/ppermute | solution.py:12
  21.2 191.3 %collective-permute-done.2 = s32[768]{0:T(1024)S(1)} collective-permute-done((s32[768]{0:T(1024)S(1)}, s32[768]{0:T(1024)S(1)}, u32[]{:S(2)}, u32[]{:S(2)}) %collective-permute-start.2) | collective-permute-done | bytes 3104 | tf_op jit(solution)/shard_map/ppermute | solution.py:12
  212.6 27.7 %collective-permute-done = s32[768]{0:T(1024)S(1)} collective-permute-done((s32[768]{0:T(1024)S(1)}, s32[768]{0:T(1024)S(1)}, u32[]{:S(2)}, u32[]{:S(2)}) %collective-permute-start) | collective-permute-done | bytes 3104 | tf_op jit(solution)/shard_map/ppermute | solution.py:12
  240.2 0.0 collective-permute-done.3
  240.3 5.2 %fusion.7 = f32[768,768]{0,1:T(8,128)S(1)} fusion(bf16[768,4096]{1,0:T(8,128)(2,1)S(1)} %fusion.1, bf16[768,4096]{1,0:T(8,128)(2,1)S(1)} %collective-permute-done.3), kind=kOutput, calls=%fused_computation.18 | convolution fusion | flops 4831838208 | bytes 14942208 | tf_op jit(solution)/shard_map/dot_general | solution.py:23
  245.5 0.0 collective-permute-done.1
  245.5 5.6 %fusion.4 = (f32[768]{0:T(1024)S(1)}, f32[768]{0:T(1024)S(1)}, f32[768]{0:T(1024)S(1)}, f32[768]{0:T(1024)S(1)}) fusion(s32[768]{0:T(1024)S(1)} %copy-done.1, s32[768]{0:T(1024)S(1)} %broadcast_add_fusion.1, f32[768,768]{0,1:T(8,128)S(1)} %fusion.7, s32[768]{0:T(1024)S(1)} %broadcast_add_fusion, bf16[768,4096]{1,0:T(8,128)(2,1)S(1)} %fusion.1, ...), kind=kOutput, calls=%fused_computation.10 | convolution fusion | flops 4837732352 | bytes 14963712 | tf_op jit(solution)/shard_map/dot_general | solution.py:23
  251.1 45.8 %collective-permute-start.4 = (f32[768]{0:T(1024)S(1)}, f32[768]{0:T(1024)S(1)}, u32[]{:S(2)}, u32[]{:S(2)}) collective-permute-start(f32[768]{0:T(1024)S(1)} %get-tuple-element.6), channel_id=1, source_target_pairs={{0,1},{1,2},{2,3},{3,4},{4,5},{5,6},{6,7},{7,8},{8,9},{9,10},{10,1... | collective-permute-start | bytes 9224 | tf_op jit(solution)/shard_map/ppermute | solution.py:12
  296.9 27.3 %collective-permute-start.5 = (f32[768]{0:T(1024)S(1)}, f32[768]{0:T(1024)S(1)}, u32[]{:S(2)}, u32[]{:S(2)}) collective-permute-start(f32[768]{0:T(1024)S(1)} %get-tuple-element.9), channel_id=1, source_target_pairs={{0,2},{1,3},{2,4},{3,5},{4,6},{5,7},{6,8},{7,9},{8,10},{9,11},{10,... | collective-permute-start | bytes 9224 | tf_op jit(solution)/shard_map/ppermute | solution.py:12
  324.3 5.3 %select_reduce_fusion = f32[768]{0:T(1024)S(1)} fusion(bf16[768,4096]{1,0:T(8,128)(2,1)S(1)} %fusion.1, s32[768]{0:T(1024)S(1)} %copy-done.1), kind=kOutput, calls=%fused_computation.6 | convolution fusion | flops 4835376128 | bytes 6297600 | tf_op jit(solution)/shard_map/dot_general | solution.py:33
  329.6 0.0 collective-permute-done.4
  329.6 0.0 collective-permute-done.5
  329.6 0.6 maximum_add_fusion
  (4 shorter events, 0.0 us)
Async XLA Ops:
  0.0 4.6 %copy-start = (bf16[768,4096]{1,0:T(8,128)(2,1)S(1)}, bf16[768,4096]{1,0:T(8,128)(2,1)}, u32[]{:S(2)}) copy-start(bf16[768,4096]{1,0:T(8,128)(2,1)} %param.2) | copy-start | bytes 18874372
  4.6 9.0 %copy-start.1 = (s32[768]{0:T(1024)S(1)}, s32[768]{0:T(1024)}, u32[]{:S(2)}) copy-start(s32[768]{0:T(1024)} %param.3) | copy-start | bytes 9220
  6.9 233.3 %collective-permute-start.3 = (bf16[768,4096]{1,0:T(8,128)(2,1)S(1)}, bf16[768,4096]{1,0:T(8,128)(2,1)S(1)}, u32[]{:S(2)}, u32[]{:S(2)}) collective-permute-start(bf16[768,4096]{1,0:T(8,128)(2,1)S(1)} %fusion.1), channel_id=1, source_target_pairs={{2,0},{3,1},{4,2},{5,3},{6,4},{7,5},{8,6},{9,7},{10,8},{11,9},{12,... | collective-permute-start | bytes 18874376 | tf_op jit(solution)/shard_map/ppermute | solution.py:12
  10.9 234.6 %collective-permute-start.1 = (bf16[768,4096]{1,0:T(8,128)(2,1)S(1)}, bf16[768,4096]{1,0:T(8,128)(2,1)S(1)}, u32[]{:S(2)}, u32[]{:S(2)}) collective-permute-start(bf16[768,4096]{1,0:T(8,128)(2,1)S(1)} %fusion.1), channel_id=1, source_target_pairs={{1,0},{2,1},{3,2},{4,3},{5,4},{6,5},{7,6},{8,7},{9,8},{10,9},{11,1... | collective-permute-start | bytes 18874376 | tf_op jit(solution)/shard_map/ppermute | solution.py:12
  13.7 198.9 %collective-permute-start.2 = (s32[768]{0:T(1024)S(1)}, s32[768]{0:T(1024)S(1)}, u32[]{:S(2)}, u32[]{:S(2)}) collective-permute-start(s32[768]{0:T(1024)S(1)} %broadcast_add_fusion.2), channel_id=1, source_target_pairs={{2,0},{3,1},{4,2},{5,3},{6,4},{7,5},{8,6},{9,7},{10,8},{11,9},{12,... | collective-permute-start | bytes 9224 | tf_op jit(solution)/shard_map/ppermute | solution.py:12
  17.4 222.9 %collective-permute-start = (s32[768]{0:T(1024)S(1)}, s32[768]{0:T(1024)S(1)}, u32[]{:S(2)}, u32[]{:S(2)}) collective-permute-start(s32[768]{0:T(1024)S(1)} %broadcast_add_fusion.2), channel_id=1, source_target_pairs={{1,0},{2,1},{3,2},{4,3},{5,4},{6,5},{7,6},{8,7},{9,8},{10,9},{11,1... | collective-permute-start | bytes 9224 | tf_op jit(solution)/shard_map/ppermute | solution.py:12
  251.1 78.4 %collective-permute-start.4 = (f32[768]{0:T(1024)S(1)}, f32[768]{0:T(1024)S(1)}, u32[]{:S(2)}, u32[]{:S(2)}) collective-permute-start(f32[768]{0:T(1024)S(1)} %get-tuple-element.6), channel_id=1, source_target_pairs={{0,1},{1,2},{2,3},{3,4},{4,5},{5,6},{6,7},{7,8},{8,9},{9,10},{10,1... | collective-permute-start | bytes 9224 | tf_op jit(solution)/shard_map/ppermute | solution.py:12
  296.9 32.7 %collective-permute-start.5 = (f32[768]{0:T(1024)S(1)}, f32[768]{0:T(1024)S(1)}, u32[]{:S(2)}, u32[]{:S(2)}) collective-permute-start(f32[768]{0:T(1024)S(1)} %get-tuple-element.9), channel_id=1, source_target_pairs={{0,2},{1,3},{2,4},{3,5},{4,6},{5,7},{6,8},{7,9},{8,10},{9,11},{10,... | collective-permute-start | bytes 9224 | tf_op jit(solution)/shard_map/ppermute | solution.py:12
where the time goes:
time: 330 us
  waiting for transfers between devices  219 us (66%)
  starting transfers between devices  87.3 us (26%)
  matrix products  16.2 us (5%)
  other arithmetic  7.17 us (2%)
    ppermute x6, waiting for transfers between devices, passed_along(): return lax.ppermute(block, axis, route)  219 us
    ppermute x6, starting transfers between devices, passed_along(): return lax.ppermute(block, axis, route)  87.3 us
    dot_general x2, matrix products, lifted_tile(): scores = jnp.dot(own, other.T, preferred_element_type=jnp.float32) + 1.0  10.9 us
  transfers between devices with their start and end apart: 6, of which 2 were waited for; matrix products, arithmetic and copies ran while one was open for 3% of the time, Pallas kernels for 0%

commit v1 on v0

v1 whole, which is shorter than its diff:
```python
import jax
import jax.numpy as jnp
from jax import lax
from jax.experimental import pallas as pl
from jax.experimental.pallas import tpu as pltpu
from jax.sharding import PartitionSpec as P

MESH = pl.DeviceIdType.MESH
CHUNK = 64
SLAB = 16


def scores_of(rows, columns):
    return 1.0 + lax.dot_general(
        rows, columns, (((1,), (1,)), ((), ())), preferred_element_type=jnp.float32
    )


def kernel(
    devices, inner,
    x_ref, ids_ref, out_ref,
    raw, unit, left, right, ids_in, ids_col, ret_out, ret_in, best, wide_a, wide_c,
    raw_sem, send_l, send_r, recv_l, recv_r, ids_send, ids_recv, ret_send, ret_recv,
):
    count, width = x_ref.shape
    steps = count // CHUNK
    half = steps // 2
    mid = count // 2
    me = lax.axis_index("pieces") * inner + lax.axis_index("grp")
    after, before = lax.rem(me + 1, devices), lax.rem(me + devices - 1, devices)
    to_after = (after // inner, lax.rem(after, inner))
    to_before = (before // inner, lax.rem(before, inner))

    def rows_of(chunk):
        return pl.ds(pl.multiple_of(chunk * CHUNK, CHUNK), CHUNK)

    def load(chunk):
        return pltpu.make_async_copy(
            x_ref.at[rows_of(chunk)], raw.at[rows_of(chunk)], raw_sem.at[chunk]
        )

    def to_right(step):
        rows = rows_of(steps - 1 - step)
        return pltpu.make_async_remote_copy(
            src_ref=unit.at[rows], dst_ref=left.at[rows],
            send_sem=send_r.at[step], recv_sem=recv_l.at[step],
            device_id=to_after, device_id_type=MESH,
        )

    def to_left(step):
        rows = rows_of(step)
        return pltpu.make_async_remote_copy(
            src_ref=unit.at[rows], dst_ref=right.at[rows],
            send_sem=send_l.at[step], recv_sem=recv_r.at[step],
            device_id=to_before, device_id_type=MESH,
        )

    def small(source, landing, sems, slot, target):
        return pltpu.make_async_remote_copy(
            src_ref=source, dst_ref=landing, send_sem=sems[0].at[slot],
            recv_sem=sems[1].at[slot], device_id=target, device_id_type=MESH,
        )

    @pl.loop(0, half)
    def _(k):
        load(k).start()
        load(steps - 1 - k).start()

    barrier = pltpu.get_barrier_semaphore()
    for target in (to_after, to_before):
        pl.semaphore_signal(barrier, inc=1, device_id=target, device_id_type=MESH)
    pl.semaphore_wait(barrier, 2)

    ids_after = small(ids_ref, ids_in.at[0], (ids_send, ids_recv), 0, to_after)
    ids_before = small(ids_ref, ids_in.at[1], (ids_send, ids_recv), 1, to_before)
    ids_after.start()
    ids_before.start()

    def normalize(chunk):
        load(chunk).wait()

        @pl.loop(0, CHUNK // SLAB)
        def _(slab):
            rows = pl.ds(pl.multiple_of(chunk * CHUNK + slab * SLAB, SLAB), SLAB)
            wide = raw[rows, :].astype(jnp.float32)
            scale = lax.rsqrt(jnp.sum(wide * wide, axis=1, keepdims=True) + 1e-06)
            unit[rows, :] = (wide * scale).astype(jnp.bfloat16)

    @pl.loop(0, half)
    def _(k):
        normalize(k)
        to_left(k).start()
        normalize(steps - 1 - k)
        to_right(k).start()

    own_ids = ids_ref[0:1, :]
    best[...] = jnp.zeros_like(best)
    ret_out[...] = jnp.zeros_like(ret_out)
    ids_col[2] = jnp.transpose(jnp.broadcast_to(own_ids, (128, count)))

    def raise_best(value):
        best[0:1, :] = jnp.maximum(best[0:1, :], jnp.max(value, axis=0, keepdims=True))

    @pl.loop(0, steps)
    def _(chunk):
        rows = rows_of(chunk)
        scores = scores_of(unit[rows, :], unit[...])
        place = chunk * CHUNK + lax.broadcasted_iota(jnp.int32, scores.shape, 0)
        other = place != lax.broadcasted_iota(jnp.int32, scores.shape, 1)
        keep = (ids_col[2, rows, 0:1] == own_ids) & other
        raise_best(jnp.where(keep, scores, 0.0))

    ids_after.wait()
    ids_before.wait()
    for side in range(2):
        ids_col[side] = jnp.transpose(jnp.broadcast_to(ids_in[side, 0:1, :], (128, count)))

    def folded(value):
        wide = value[:, 0:128]
        for at in range(128, mid, 128):
            wide = jnp.maximum(wide, value[:, at:at + 128])
        return wide

    def outer(rows, row_buf, row_side, col_buf, col_side, cols, wide, wide_rows):
        scores = scores_of(row_buf[rows, :], col_buf[cols, :])
        keep = ids_col[row_side, rows, 0:1] == ids_in[col_side, 0:1, cols]
        lifted = jnp.where(keep, scores, 0.0)
        found = jnp.max(lifted, axis=0, keepdims=True)
        ret_out[col_side, 0:1, cols] = jnp.maximum(ret_out[col_side, 0:1, cols], found)
        if wide is not None:
            wide[wide_rows, :] = folded(lifted)
        return lifted

    near_l, near_r = slice(mid, count), slice(0, mid)

    @pl.loop(0, steps)
    def _(step):
        to_right(step).wait()
        to_left(step).wait()

        @pl.when(step < half)
        def _():
            to_right(step + half).start()
            to_left(step + half).start()

        rows_l, rows_r = rows_of(steps - 1 - step), rows_of(step)

        @pl.when(step >= half)
        def _():
            at = pl.ds(pl.multiple_of((step - half) * CHUNK, CHUNK), CHUNK)
            from_l = pl.ds(pl.multiple_of((steps - 1 - step) * CHUNK, CHUNK), CHUNK)
            outer(rows_l, left, 0, right, 1, near_r, wide_a, from_l)
            outer(rows_r, right, 1, left, 0, near_l, wide_c, at)

        @pl.when(step == half - 1)
        def _():
            @pl.loop(0, half)
            def _(k):
                outer(rows_of(k), right, 1, left, 0, near_l, None, None)
                outer(rows_of(steps - 1 - k), left, 0, right, 1, near_r, None, None)

        scores = scores_of(left[rows_l, :], unit[...])
        raise_best(jnp.where(ids_col[0, rows_l, 0:1] == own_ids, scores, 0.0))
        scores = scores_of(right[rows_r, :], unit[...])
        raise_best(jnp.where(ids_col[1, rows_r, 0:1] == own_ids, scores, 0.0))

    ret_out[0, 0:1, 0:mid] = jnp.max(jnp.transpose(wide_a[...]), axis=0, keepdims=True)
    ret_out[1, 0:1, mid:count] = jnp.max(jnp.transpose(wide_c[...]), axis=0, keepdims=True)
    back_before = small(ret_out.at[0], ret_in.at[0], (ret_send, ret_recv), 0, to_before)
    back_after = small(ret_out.at[1], ret_in.at[1], (ret_send, ret_recv), 1, to_after)
    back_before.start()
    back_after.start()
    back_before.wait()
    back_after.wait()
    out_ref[...] = jnp.maximum(jnp.maximum(ret_in[0], ret_in[1]), best[...]) - 1.0


def solution(mesh):
    devices, inner = mesh.size, mesh.shape["grp"]

    def shards(embeddings, cluster_ids):
        count, width = embeddings.shape
        steps = count // CHUNK
        ids = jnp.broadcast_to(cluster_ids[None, :], (8, count))
        rows = pltpu.VMEM((count, width), jnp.bfloat16)
        sems = pltpu.SemaphoreType.DMA
        found = pl.pallas_call(
            lambda *refs: kernel(devices, inner, *refs),
            out_shape=jax.ShapeDtypeStruct((8, count), jnp.float32),
            in_specs=[
                pl.BlockSpec(memory_space=pl.ANY),
                pl.BlockSpec(memory_space=pltpu.VMEM),
            ],
            out_specs=pl.BlockSpec(memory_space=pltpu.VMEM),
            scratch_shapes=[
                rows, rows, rows, rows,
                pltpu.VMEM((2, 8, count), jnp.int32),
                pltpu.VMEM((3, count, 128), jnp.int32),
                pltpu.VMEM((2, 8, count), jnp.float32),
                pltpu.VMEM((2, 8, count), jnp.float32),
                pltpu.VMEM((8, count), jnp.float32),
                pltpu.VMEM((count // 2, 128), jnp.float32),
                pltpu.VMEM((count // 2, 128), jnp.float32),
                sems((steps,)), sems((steps,)), sems((steps,)), sems((steps,)), sems((steps,)),
                sems((2,)), sems((2,)), sems((2,)), sems((2,)),
            ],
            compiler_params=pltpu.CompilerParams(
                collective_id=0, has_side_effects=True, vmem_limit_bytes=58 * 1024 * 1024
            ),
            cost_estimate=pl.CostEstimate(
                flops=9 * count * count * width, bytes_accessed=2 * count * width,
                transcendentals=count,
            ),
        )(embeddings, ids)
        return found[0]

    return jax.shard_map(
        shards,
        mesh=mesh,
        in_specs=(P(("pieces", "grp"), None), P(("pieces", "grp"))),
        out_specs=P(("pieces", "grp")),
        check_vma=False,
    )
```

time: 330 us -> 169 us (0.51)
  the two profiles are of different devices: /device:TPU:96 before, /device:TPU:1 now
where the time goes in v1:
time: 169 us
  Pallas kernels  166 us (98%)
  local copies, waits for them, and re-layouts  2.62 us (2%)
    pallas_call x1, Pallas kernels, shards(): pl.pallas_call(lambda *refs: kernel(devices, inner, *refs), out_shape=jax...  166 us

profile of v1, /device:TPU:1, one launch (start us, length us, event | category | flops | bytes accessed | tf_op | source)
XLA Modules:
  0.0 168.6 jit_solution(1491087421355020628)
XLA Ops:
  0.0 1.3 broadcast_in_dim.2.refs_1_
  1.3 166.0 %shard_map.28 = f32[8,768]{1,0:T(8,128)} custom-call(bf16[768,4096]{1,0:T(8,128)(2,1)} %refs_0_.1, s32[8,768]{1,0:T(8,128)} %broadcast_in_dim.2.refs_1_), custom_call_target="tpu_custom_call" | custom-call | flops 21743271936 | bytes 6291456 | tf_op jit(solution)/shard_map/pallas_call | solution.py:187
  167.3 1.3 slice_reduce_fusion

commit v2 on v1

--- a/solution.py
+++ b/solution.py
@@ -8,6 +8,10 @@
 MESH = pl.DeviceIdType.MESH
 CHUNK = 64
 SLAB = 16
+BLOCK = 256
+AHEAD = 6
+MIDDLE, LATE = 512, 640
+BLOCKS = ((0, 256, 0), (256, 512, 0), (512, 640, 256), (640, 704, 128), (704, 768, 128))
 
 
 def scores_of(rows, columns):
@@ -25,7 +29,6 @@
     count, width = x_ref.shape
     steps = count // CHUNK
     half = steps // 2
-    mid = count // 2
     me = lax.axis_index("pieces") * inner + lax.axis_index("grp")
     after, before = lax.rem(me + 1, devices), lax.rem(me + devices - 1, devices)
     to_after = (after // inner, lax.rem(after, inner))
@@ -101,11 +104,11 @@
     def raise_best(value):
         best[0:1, :] = jnp.maximum(best[0:1, :], jnp.max(value, axis=0, keepdims=True))
 
-    @pl.loop(0, steps)
-    def _(chunk):
-        rows = rows_of(chunk)
+    @pl.loop(0, count // BLOCK)
+    def _(block):
+        rows = pl.ds(pl.multiple_of(block * BLOCK, BLOCK), BLOCK)
         scores = scores_of(unit[rows, :], unit[...])
-        place = chunk * CHUNK + lax.broadcasted_iota(jnp.int32, scores.shape, 0)
+        place = block * BLOCK + lax.broadcasted_iota(jnp.int32, scores.shape, 0)
         other = place != lax.broadcasted_iota(jnp.int32, scores.shape, 1)
         keep = (ids_col[2, rows, 0:1] == own_ids) & other
         raise_best(jnp.where(keep, scores, 0.0))
@@ -115,61 +118,57 @@
     for side in range(2):
         ids_col[side] = jnp.transpose(jnp.broadcast_to(ids_in[side, 0:1, :], (128, count)))
 
-    def folded(value):
-        wide = value[:, 0:128]
-        for at in range(128, mid, 128):
-            wide = jnp.maximum(wide, value[:, at:at + 128])
-        return wide
-
-    def outer(rows, row_buf, row_side, col_buf, col_side, cols, wide, wide_rows):
-        scores = scores_of(row_buf[rows, :], col_buf[cols, :])
+    def outer(rows, row_side, cols, col_side, wide):
+        buffers = (left, right)
+        scores = scores_of(buffers[row_side][rows, :], buffers[col_side][cols, :])
         keep = ids_col[row_side, rows, 0:1] == ids_in[col_side, 0:1, cols]
         lifted = jnp.where(keep, scores, 0.0)
         found = jnp.max(lifted, axis=0, keepdims=True)
         ret_out[col_side, 0:1, cols] = jnp.maximum(ret_out[col_side, 0:1, cols], found)
-        if wide is not None:
-            wide[wide_rows, :] = folded(lifted)
-        return lifted
-
-    near_l, near_r = slice(mid, count), slice(0, mid)
-
-    @pl.loop(0, steps)
-    def _(step):
-        to_right(step).wait()
-        to_left(step).wait()
-
-        @pl.when(step < half)
-        def _():
-            to_right(step + half).start()
-            to_left(step + half).start()
-
-        rows_l, rows_r = rows_of(steps - 1 - step), rows_of(step)
-
-        @pl.when(step >= half)
-        def _():
-            at = pl.ds(pl.multiple_of((step - half) * CHUNK, CHUNK), CHUNK)
-            from_l = pl.ds(pl.multiple_of((steps - 1 - step) * CHUNK, CHUNK), CHUNK)
-            outer(rows_l, left, 0, right, 1, near_r, wide_a, from_l)
-            outer(rows_r, right, 1, left, 0, near_l, wide_c, at)
-
-        @pl.when(step == half - 1)
-        def _():
-            @pl.loop(0, half)
-            def _(k):
-                outer(rows_of(k), right, 1, left, 0, near_l, None, None)
-                outer(rows_of(steps - 1 - k), left, 0, right, 1, near_r, None, None)
-
-        scores = scores_of(left[rows_l, :], unit[...])
-        raise_best(jnp.where(ids_col[0, rows_l, 0:1] == own_ids, scores, 0.0))
-        scores = scores_of(right[rows_r, :], unit[...])
-        raise_best(jnp.where(ids_col[1, rows_r, 0:1] == own_ids, scores, 0.0))
-
-    ret_out[0, 0:1, 0:mid] = jnp.max(jnp.transpose(wide_a[...]), axis=0, keepdims=True)
-    ret_out[1, 0:1, mid:count] = jnp.max(jnp.transpose(wide_c[...]), axis=0, keepdims=True)
+        fold = lifted[:, 0:128]
+        for at in range(128, lifted.shape[1], 128):
+            fold = jnp.maximum(fold, lifted[:, at:at + 128])
+        wide[rows, :] = fold
+
+    def found_rows(side, wide, rows):
+        found = jnp.max(jnp.transpose(wide[rows, :]), axis=0, keepdims=True)
+        ret_out[side, 0:1, rows] = jnp.maximum(ret_out[side, 0:1, rows], found)
+
+    def own_part(rows_l, rows_r):
+        scores = scores_of(jnp.concatenate([left[rows_l, :], right[rows_r, :]]), unit[...])
+        ids = jnp.concatenate([ids_col[0, rows_l, 0:1], ids_col[1, rows_r, 0:1]])
+        raise_best(jnp.where(ids == own_ids, scores, 0.0))
+
+    for start, stop, near in BLOCKS:
+        @pl.loop(start // CHUNK, stop // CHUNK)
+        def _(step):
+            to_right(step).wait()
+            to_left(step).wait()
+
+            @pl.when(step + AHEAD < steps)
+            def _():
+                to_right(step + AHEAD).start()
+                to_left(step + AHEAD).start()
+
+        rows_l, rows_r = slice(count - stop, count - start), slice(start, stop)
+        if near:
+            outer(rows_l, 0, slice(0, near), 1, wide_a)
+            outer(rows_r, 1, slice(count - near, count), 0, wide_c)
+        if stop == MIDDLE:
+            outer(slice(0, stop), 1, slice(count - stop, count), 0, wide_c)
+        if stop == LATE:
+            found_rows(0, wide_a, slice(128, count - MIDDLE))
+            found_rows(1, wide_c, slice(0, LATE))
+        if stop < count:
+            own_part(rows_l, rows_r)
+
+    found_rows(0, wide_a, slice(0, count - LATE))
+    found_rows(1, wide_c, slice(LATE, count))
     back_before = small(ret_out.at[0], ret_in.at[0], (ret_send, ret_recv), 0, to_before)
     back_after = small(ret_out.at[1], ret_in.at[1], (ret_send, ret_recv), 1, to_after)
     back_before.start()
     back_after.start()
+    own_part(rows_l, rows_r)
     back_before.wait()
     back_after.wait()
     out_ref[...] = jnp.maximum(jnp.maximum(ret_in[0], ret_in[1]), best[...]) - 1.0
@@ -199,8 +198,8 @@
                 pltpu.VMEM((2, 8, count), jnp.float32),
                 pltpu.VMEM((2, 8, count), jnp.float32),
                 pltpu.VMEM((8, count), jnp.float32),
-                pltpu.VMEM((count // 2, 128), jnp.float32),
-                pltpu.VMEM((count // 2, 128), jnp.float32),
+                pltpu.VMEM((count - MIDDLE, 128), jnp.float32),
+                pltpu.VMEM((count, 128), jnp.float32),
                 sems((steps,)), sems((steps,)), sems((steps,)), sems((steps,)), sems((steps,)),
                 sems((2,)), sems((2,)), sems((2,)), sems((2,)),
             ],

time: 169 us -> 154 us (0.911)
  the two profiles are of different devices: /device:TPU:1 before, /device:TPU:0 now
where the time goes in v2:
time: 154 us
  Pallas kernels  151 us (98%)
  local copies, waits for them, and re-layouts  2.62 us (2%)
    pallas_call x1, Pallas kernels, shards(): pl.pallas_call(lambda *refs: kernel(devices, inner, *refs), out_shape=jax...  151 us

profile of v2, /device:TPU:0, one launch (start us, length us, event | category | flops | bytes accessed | tf_op | source)
XLA Modules:
  0.0 153.7 jit_solution(14417026892516580293)
XLA Ops:
  0.0 1.3 broadcast_in_dim.2.refs_1_
  1.3 151.1 %shard_map.28 = f32[8,768]{1,0:T(8,128)} custom-call(bf16[768,4096]{1,0:T(8,128)(2,1)} %refs_0_.1, s32[8,768]{1,0:T(8,128)} %broadcast_in_dim.2.refs_1_), custom_call_target="tpu_custom_call" | custom-call | flops 21743271936 | bytes 6291456 | tf_op jit(solution)/shard_map/pallas_call | solution.py:186
  152.4 1.3 slice_reduce_fusion

commit v3 on v0

v3 whole, which is shorter than its diff:
```python
import jax
import jax.numpy as jnp
from jax import lax
from jax.experimental import pallas as pl
from jax.experimental.pallas import tpu as pltpu
from jax.sharding import PartitionSpec as P

MESH = pl.DeviceIdType.MESH
CHUNK = 64
SLAB = 16
PART = 256
LATE = 128
STEPS = 2 * PART // CHUNK
AHEAD = 6
LOW, MID, TOP = slice(0, PART), slice(PART, 2 * PART), slice(2 * PART, 3 * PART)
LOWER, UPPER = slice(0, 2 * PART), slice(PART, 3 * PART)
FOURTH = slice(3 * PART, 4 * PART)


def dot(rows, columns):
    return lax.dot_general(
        rows, columns, (((1,), (1,)), ((), ())), preferred_element_type=jnp.float32
    )


def lift(scores, row_ids, col_ids):
    return jnp.where(row_ids == col_ids, 1.0 + scores, 0.0)


def by_column(lifted):
    return jnp.max(lifted, axis=0, keepdims=True)


def by_row(lifted):
    fold = lifted[:, 0:128]
    for at in range(128, lifted.shape[1], 128):
        fold = jnp.maximum(fold, lifted[:, at:at + 128])
    return fold


def raised(ref, value, *where):
    ref[where] = jnp.maximum(ref[where], value)


def kernel(
    devices, inner,
    x_ref, ids_ref, out_ref,
    raw, u1, u2, l1, l2, r1, r2, to_r, to_l, s1, s2, oo, sa1, sd1, sa2, sd2,
    part_r, part_l, from_l, from_r, ids_in, own_col, l_col, a_col, full_l, full_r,
    best, wide_own, wide_l, wide_ll, ret_out, ret_in,
    raw_sem, send_r, send_l, recv_l, recv_r, part_send, part_recv,
    ids_send, ids_recv, ret_send, ret_recv,
):
    count, width = x_ref.shape
    chunks = count // CHUNK
    h1, h2 = slice(0, width // 2), slice(width // 2, width)
    me = lax.axis_index("pieces") * inner + lax.axis_index("grp")

    def device(distance):
        index = lax.rem(me + devices + distance, devices)
        return (index // inner, lax.rem(index, inner))

    prev1, next1, prev2, next2 = device(-1), device(1), device(-2), device(2)

    def rows_of(chunk):
        return pl.ds(pl.multiple_of(chunk * CHUNK, CHUNK), CHUNK)

    def load(chunk):
        return pltpu.make_async_copy(
            x_ref.at[rows_of(chunk)], raw.at[rows_of(chunk)], raw_sem.at[chunk]
        )

    def remote(source, landing, send, recv, target):
        return pltpu.make_async_remote_copy(
            src_ref=source, dst_ref=landing, send_sem=send, recv_sem=recv,
            device_id=target, device_id_type=MESH,
        )

    def right_step(step):
        return remote(
            u1.at[rows_of(chunks - 1 - step)], l1.at[rows_of(STEPS - 1 - step)],
            send_r.at[step], recv_l.at[step], next1,
        )

    def left_step(step):
        rows = rows_of(step)
        return remote(u2.at[rows], r2.at[rows], send_l.at[step], recv_r.at[step], prev1)

    def right_part(slot, rows):
        return remote(to_r.at[rows], l2.at[rows], send_r.at[slot], recv_l.at[slot], next1)

    def left_part(slot, rows):
        return remote(to_l.at[rows], r1.at[rows], send_l.at[slot], recv_r.at[slot], prev1)

    near_r, near_l = right_part(STEPS, MID), left_part(STEPS, LOW)
    late = [slice(at, at + LATE) for at in range(0, PART, LATE)]
    far_r = [right_part(STEPS + 1 + c, rows) for c, rows in enumerate(late)]
    far_l = [
        left_part(STEPS + 1 + c, slice(PART + rows.start, PART + rows.stop))
        for c, rows in enumerate(late)
    ]
    sums_r = remote(part_r, from_l, part_send.at[0], part_recv.at[0], next1)

    def sums_left(slot, rows):
        return remote(
            part_l.at[rows], from_r.at[rows], part_send.at[slot], part_recv.at[slot], prev1
        )

    sums_l = sums_left(1, slice(0, 3 * PART))
    sums_late = [
        sums_left(2 + c, slice(3 * PART + rows.start, 3 * PART + rows.stop))
        for c, rows in enumerate(late)
    ]

    @pl.loop(0, chunks // 2)
    def _(k):
        load(k).start()
        load(chunks - 1 - k).start()

    barrier = pltpu.get_barrier_semaphore()
    for target in (prev1, next1, prev2, next2):
        pl.semaphore_signal(barrier, inc=1, device_id=target, device_id_type=MESH)
    pl.semaphore_wait(barrier, 4)

    ids_out = [
        remote(ids_ref, ids_in.at[slot], ids_send.at[slot], ids_recv.at[slot], target)
        for slot, target in enumerate((next1, prev1, next2, prev2))
    ]
    for copy in ids_out:
        copy.start()

    def normalize(chunk):
        load(chunk).wait()

        @pl.loop(0, CHUNK // SLAB)
        def _(slab):
            rows = pl.ds(pl.multiple_of(chunk * CHUNK + slab * SLAB, SLAB), SLAB)
            wide = raw[rows, :].astype(jnp.float32)
            scale = lax.rsqrt(jnp.sum(wide * wide, axis=1, keepdims=True) + 1e-06)
            unit = (wide * scale).astype(jnp.bfloat16)
            u1[rows, :] = unit[:, h1]
            u2[rows, :] = unit[:, h2]

    @pl.loop(0, AHEAD)
    def _(k):
        normalize(k)
        left_step(k).start()
        normalize(chunks - 1 - k)
        right_step(k).start()

    def ends(row):
        first, last = row[:, 0:1], row[:, count - 1:count]
        few_first = jnp.sum((row == first).astype(jnp.int32), axis=1, keepdims=True) <= 2 * PART
        few_last = jnp.sum((row == last).astype(jnp.int32), axis=1, keepdims=True) <= 2 * PART
        return first, last, few_first, few_last

    def choose(flag, yes, no, out, out_at):
        @pl.loop(0, PART // SLAB)
        def _(slab):
            def rows(at):
                return pl.ds(pl.multiple_of(at + slab * SLAB, SLAB), SLAB)

            a = yes[0][rows(yes[1]), :].astype(jnp.float32)
            b = no[0][rows(no[1]), :].astype(jnp.float32)
            out[rows(out_at), :] = jnp.where(flag, a, b).astype(jnp.bfloat16)

    def column(row):
        return jnp.transpose(jnp.broadcast_to(row, (128, row.shape[1])))

    own = ids_ref[0:1, :]
    own_first, own_last, own_few_first, own_few_last = ends(own)
    choose(own_few_last, (u2, PART), (u1, 0), to_r, 0)
    choose(own_few_first, (u1, PART), (u2, 2 * PART), to_l, PART)

    @pl.loop(0, STEPS - AHEAD)
    def _(step):
        right_step(step).wait()
        left_step(step).wait()
        right_step(step + AHEAD).start()
        left_step(step + AHEAD).start()

    for ref in (best, wide_own, wide_l, wide_ll, ret_out):
        ref[...] = jnp.zeros_like(ref)
    own_col[...] = column(own)

    @pl.loop(0, count // PART)
    def _(block):
        rows = pl.ds(pl.multiple_of(block * PART, PART), PART)
        scores = dot(u1[rows, :], u1[...]) + dot(u2[rows, :], u2[...])
        place = block * PART + lax.broadcasted_iota(jnp.int32, scores.shape, 0)
        other = place != lax.broadcasted_iota(jnp.int32, scores.shape, 1)
        lifted = jnp.where(other, lift(scores, own_col[rows, 0:1], own), 0.0)
        raised(best, by_column(lifted), slice(0, 1), slice(0, count))

    for copy in ids_out:
        copy.wait()
    l_ids, r_ids, a_ids, d_ids = (ids_in[slot, 0:1, :] for slot in range(4))
    l_first, l_last, _, l_few_last = ends(l_ids)
    r_first, r_last, r_few_first, _ = ends(r_ids)
    whole = own_first == own_last
    relay_r = whole & (l_last == own_first)
    relay_l = whole & (r_first == own_last)
    l_relays = (l_first == l_last) & (a_ids[:, count - 1:count] == l_first)
    r_relays = (r_first == r_last) & (d_ids[:, 0:1] == r_last)

    @pl.loop(STEPS - AHEAD, STEPS // 2)
    def _(step):
        right_step(step).wait()
        left_step(step).wait()

    choose(relay_r, (l1, PART), (u2, 2 * PART), to_r, PART)
    choose(relay_l, (r2, 0), (u1, 0), to_l, 0)
    near_r.start()
    near_l.start()
    l_col[...] = column(l_ids)
    a_col[...] = column(a_ids[:, TOP])
    mid_ids = jnp.where(l_few_last, l_ids[:, MID], -1)
    top_ids = jnp.where(l_relays, -1, l_ids[:, TOP])
    full_l[...] = column(jnp.concatenate([mid_ids, top_ids], axis=1))
    full_r[0:1, LOW] = jnp.where(r_relays, -2, r_ids[:, LOW])
    full_r[0:1, MID] = jnp.where(r_few_first, r_ids[:, MID], -2)

    @pl.loop(STEPS // 2, STEPS)
    def _(step):
        right_step(step).wait()
        left_step(step).wait()

    far_r[0].start()
    far_l[0].start()
    s1[UPPER, :] = dot(l1[...], u1[...])
    s2[:, LOWER] = dot(u2[...], r2[...])

    near_r.wait()
    near_l.wait()
    far_r[1].start()
    far_l[1].start()

    sa = dot(l2[MID, :], u1[UPPER, :])
    sa1[...] = sa[:, LOW]
    oo[:, LOW] = dot(l1[...], r1[LOW, :])
    part_l[LOW, :] = s1[MID, TOP]
    part_l[MID, :] = jnp.where(l_relays, s1[TOP, TOP], s1[MID, LOW])
    part_l[TOP, :] = jnp.where(l_relays, sa[:, MID], oo[LOW, LOW])
    sums_l.start()
    near_near = dot(l2[MID, :], r2[...])
    sd = dot(u2[LOWER, :], r1[LOW, :])
    sd2[...] = sd[MID, :]
    part_r[LOWER, :] = s2[LOWER, MID]
    part_r[TOP, :] = jnp.where(relay_r, s2[TOP, MID], s2[LOW, LOW])
    part_r[FOURTH, :] = jnp.where(relay_r, near_near[:, MID], sd[LOW, :])
    sums_r.start()
    oo[MID, LOW] = oo[MID, LOW] + near_near[:, LOW]
    oo[MID, MID] = near_near[:, MID]
    oo[LOW, MID] = jnp.zeros((PART, PART), jnp.float32)

    def left_found(rows, scores, row_ids):
        lifted = lift(scores, row_ids, own)
        raised(best, by_column(lifted), slice(0, 1), slice(0, count))
        raised(wide_l, by_row(lifted), rows)

    def right_found(cols, scores, col_ids):
        lifted = lift(scores, own_col[:, 0:1], col_ids)
        raised(wide_own, by_row(lifted), slice(0, count))
        raised(ret_out, by_column(lifted), 1, slice(0, 1), cols)

    left_found(TOP, s1[TOP, :] + dot(l2[MID, :], u2[...]), full_l[MID, 0:1])
    right_found(LOW, s2[:, LOW] + dot(u1[...], r1[LOW, :]), full_r[0:1, LOW])

    for c, rows in enumerate(late):
        far_r[c].wait()
        far_l[c].wait()
        above = slice(PART + rows.start, PART + rows.stop)
        beyond = slice(2 * PART + rows.start, 2 * PART + rows.stop)
        far = dot(l2[rows, :], u1[...])
        part_l[slice(3 * PART + rows.start, 3 * PART + rows.stop), :] = far[:, TOP]
        sums_late[c].start()
        s1[rows, :] = far
        s2[:, beyond] = dot(u2[...], r1[above, :])
        sd1[rows, :] = dot(l2[rows, :], r1[LOW, :])
        sa2[:, rows] = dot(l2[MID, :], r1[above, :])
        left_found(above, s1[above, :] + dot(l2[rows, :], u2[...]), full_l[rows, 0:1])
        right_found(above, s2[:, above] + dot(u1[...], r1[above, :]), full_r[0:1, above])
        oo[rows, :] = oo[rows, :] + dot(l2[rows, :], r2[...])
        oo[:, above] = oo[:, above] + dot(l1[...], r1[above, :])

    lifted = lift(oo[...], full_l[:, 0:1], full_r[0:1, :])
    raised(wide_l, by_row(lifted), UPPER)
    raised(ret_out, by_column(lifted), 1, slice(0, 1), LOWER)

    def either(flag, value, yes, no):
        raised(yes[0], jnp.where(flag, value, 0.0), *yes[1:])
        raised(no[0], jnp.where(flag, 0.0, value), *no[1:])

    one = slice(0, 1)
    sums_r.wait()
    lifted = lift(s1[LOWER, MID] + from_l[LOWER, :], l_col[LOWER, 0:1], own[:, MID])
    raised(best, by_column(lifted), one, MID)
    raised(wide_l, by_row(lifted), LOWER)
    lifted = lift(
        jnp.where(l_relays, s1[TOP, MID], s1[LOW, LOW]) + from_l[TOP, :],
        jnp.where(l_relays, l_col[TOP, 0:1], l_col[LOW, 0:1]),
        jnp.where(l_relays, own[:, MID], own[:, LOW]),
    )
    either(l_relays, by_column(lifted), (best, one, MID), (best, one, LOW))
    either(l_relays, by_row(lifted), (wide_l, TOP), (wide_l, LOW))
    lifted = lift(
        jnp.where(l_relays, sa1[...], sd1[...]) + from_l[FOURTH, :],
        jnp.where(l_relays, a_col[:, 0:1], l_col[LOW, 0:1]),
        jnp.where(l_relays, own[:, MID], r_ids[:, LOW]),
    )
    either(l_relays, by_column(lifted), (best, one, MID), (ret_out, 1, one, LOW))
    either(l_relays, by_row(lifted), (wide_ll, LOW), (wide_l, LOW))

    sums_l.wait()
    lifted = lift(
        jnp.where(relay_r, s2[TOP, TOP], s2[MID, LOW]) + from_r[MID, :],
        jnp.where(relay_r, own_col[TOP, 0:1], own_col[MID, 0:1]),
        jnp.where(relay_r, r_ids[:, TOP], r_ids[:, LOW]),
    )
    either(relay_r, by_column(lifted), (ret_out, 1, one, TOP), (ret_out, 1, one, LOW))
    either(relay_r, by_row(lifted), (wide_own, TOP), (wide_own, MID))
    lifted = lift(
        jnp.where(relay_r, sa2[...], sd2[...]) + from_r[TOP, :],
        jnp.where(relay_r, l_col[TOP, 0:1], own_col[MID, 0:1]),
        jnp.where(relay_r, r_ids[:, TOP], d_ids[:, LOW]),
    )
    either(relay_r, by_column(lifted), (ret_out, 1, one, TOP), (ret_out, 3, one, LOW))
    either(relay_r, by_row(lifted), (wide_l, TOP), (wide_own, MID))
    lifted = lift(s2[MID, TOP] + from_r[LOW, :], own_col[MID, 0:1], r_ids[:, TOP])
    raised(ret_out, by_column(lifted), 1, one, TOP)
    raised(wide_own, by_row(lifted), MID)
    for copy in sums_late:
        copy.wait()
    lifted = lift(s2[LOW, TOP] + from_r[FOURTH, :], own_col[LOW, 0:1], r_ids[:, TOP])
    raised(ret_out, by_column(lifted), 1, one, TOP)
    raised(wide_own, by_row(lifted), LOW)

    def across(wide):
        return by_column(jnp.transpose(wide))

    ret_out[0, 0:1, :] = across(wide_l[...])
    ret_out[2, 0:1, TOP] = across(wide_ll[...])
    back = [
        remote(ret_out.at[slot], ret_in.at[slot], ret_send.at[slot], ret_recv.at[slot], target)
        for slot, target in enumerate((prev1, next1, prev2, next2))
    ]
    for copy in back:
        copy.start()
    found = jnp.maximum(best[0:1, :], across(wide_own[...]))
    for copy in back:
        copy.wait()
    for slot in range(4):
        found = jnp.maximum(found, ret_in[slot, 0:1, :])
    out_ref[...] = jnp.broadcast_to(found - 1.0, out_ref.shape)


def solution(mesh):
    devices, inner = mesh.size, mesh.shape["grp"]

    def shards(embeddings, cluster_ids):
        count, width = embeddings.shape
        ids = jnp.broadcast_to(cluster_ids[None, :], (8, count))
        sems = pltpu.SemaphoreType.DMA

        def half_rows(rows):
            return pltpu.VMEM((rows, width // 2), jnp.bfloat16)

        def floats(*shape):
            return pltpu.VMEM(shape, jnp.float32)

        def ints(*shape):
            return pltpu.VMEM(shape, jnp.int32)

        slots = STEPS + 1 + PART // LATE
        found = pl.pallas_call(
            lambda *refs: kernel(devices, inner, *refs),
            out_shape=jax.ShapeDtypeStruct((8, count), jnp.float32),
            in_specs=[
                pl.BlockSpec(memory_space=pl.ANY),
                pl.BlockSpec(memory_space=pltpu.VMEM),
            ],
            out_specs=pl.BlockSpec(memory_space=pltpu.VMEM),
            scratch_shapes=[
                pltpu.VMEM((count, width), jnp.bfloat16),
                half_rows(count), half_rows(count),
                half_rows(2 * PART), half_rows(2 * PART), half_rows(2 * PART), half_rows(2 * PART),
                half_rows(2 * PART), half_rows(2 * PART),
                floats(count, count), floats(count, count), floats(2 * PART, 2 * PART),
                floats(PART, PART), floats(PART, PART), floats(PART, PART), floats(PART, PART),
                floats(4 * PART, PART), floats(4 * PART, PART),
                floats(4 * PART, PART), floats(4 * PART, PART),
                ints(4, 8, count), ints(count, 128), ints(count, 128), ints(PART, 128),
                ints(2 * PART, 128), ints(8, 2 * PART),
                floats(8, count), floats(count, 128), floats(count, 128), floats(PART, 128),
                floats(4, 8, count), floats(4, 8, count),
                sems((count // CHUNK,)),
                sems((slots,)), sems((slots,)), sems((slots,)), sems((slots,)),
                sems((2 + PART // LATE,)), sems((2 + PART // LATE,)),
                sems((4,)), sems((4,)), sems((4,)), sems((4,)),
            ],
            compiler_params=pltpu.CompilerParams(
                collective_id=0, has_side_effects=True, vmem_limit_bytes=60 * 1024 * 1024
            ),
            cost_estimate=pl.CostEstimate(
                flops=9 * count * count * width, bytes_accessed=2 * count * width,
                transcendentals=count,
            ),
        )(embeddings, ids)
        return found[0]

    return jax.shard_map(
        shards,
        mesh=mesh,
        in_specs=(P(("pieces", "grp"), None), P(("pieces", "grp"))),
        out_specs=P(("pieces", "grp")),
        check_vma=False,
    )
```

time: 330 us -> 134 us (0.41)
  the two profiles are of different devices: /device:TPU:96 before, /device:TPU:0 now
where the time goes in v3:
time: 134 us
  Pallas kernels  131 us (98%)
  local copies, waits for them, and re-layouts  2.62 us (2%)
    pallas_call x1, Pallas kernels, shards(): pl.pallas_call(lambda *refs: kernel(devices, inner, *refs), out_shape=jax...  131 us

profile of v3, /device:TPU:0, one launch (start us, length us, event | category | flops | bytes accessed | tf_op | source)
XLA Modules:
  0.0 133.8 jit_solution(5197135292092239834)
XLA Ops:
  0.0 1.3 broadcast_in_dim.2.refs_1_
  1.3 131.2 %shard_map.28 = f32[8,768]{1,0:T(8,128)} custom-call(bf16[768,4096]{1,0:T(8,128)(2,1)} %refs_0_.1, s32[8,768]{1,0:T(8,128)} %broadcast_in_dim.2.refs_1_), custom_call_target="tpu_custom_call" | custom-call | flops 21743271936 | bytes 6291456 | tf_op jit(solution)/shard_map/pallas_call | solution.py:375
  132.5 1.3 %slice_reduce_fusion = f32[768]{0:T(1024)} fusion(f32[8,768]{1,0:T(8,128)} %shard_map.28), kind=kLoop, calls=%fused_computation | loop fusion | bytes 6144 | tf_op jit(solution)/shard_map/slice | solution.py:409

commit v4 on v3

--- a/solution.py
+++ b/solution.py
@@ -14,7 +14,7 @@
 AHEAD = 6
 LOW, MID, TOP = slice(0, PART), slice(PART, 2 * PART), slice(2 * PART, 3 * PART)
 LOWER, UPPER = slice(0, 2 * PART), slice(PART, 3 * PART)
-FOURTH = slice(3 * PART, 4 * PART)
+HALF = PART // 2
 
 
 def dot(rows, columns):
@@ -106,9 +106,9 @@
             part_l.at[rows], from_r.at[rows], part_send.at[slot], part_recv.at[slot], prev1
         )
 
-    sums_l = sums_left(1, slice(0, 3 * PART))
+    sums_l = sums_left(1, LOWER)
     sums_late = [
-        sums_left(2 + c, slice(3 * PART + rows.start, 3 * PART + rows.stop))
+        sums_left(2 + c, slice(2 * PART + rows.start, 2 * PART + rows.stop))
         for c, rows in enumerate(late)
     ]
 
@@ -120,14 +120,6 @@
     barrier = pltpu.get_barrier_semaphore()
     for target in (prev1, next1, prev2, next2):
         pl.semaphore_signal(barrier, inc=1, device_id=target, device_id_type=MESH)
-    pl.semaphore_wait(barrier, 4)
-
-    ids_out = [
-        remote(ids_ref, ids_in.at[slot], ids_send.at[slot], ids_recv.at[slot], target)
-        for slot, target in enumerate((next1, prev1, next2, prev2))
-    ]
-    for copy in ids_out:
-        copy.start()
 
     def normalize(chunk):
         load(chunk).wait()
@@ -141,7 +133,21 @@
             u1[rows, :] = unit[:, h1]
             u2[rows, :] = unit[:, h2]
 
-    @pl.loop(0, AHEAD)
+    normalize(0)
+    normalize(chunks - 1)
+    pl.semaphore_wait(barrier, 4)
+
+    ids_out = [
+        remote(ids_ref, ids_in.at[slot], ids_send.at[slot], ids_recv.at[slot], target)
+        for slot, target in enumerate((next1, prev1, next2, prev2))
+    ]
+    for copy in ids_out:
+        copy.start()
+
+    left_step(0).start()
+    right_step(0).start()
+
+    @pl.loop(1, AHEAD)
     def _(k):
         normalize(k)
         left_step(k).start()
@@ -150,12 +156,12 @@
 
     def ends(row):
         first, last = row[:, 0:1], row[:, count - 1:count]
-        few_first = jnp.sum((row == first).astype(jnp.int32), axis=1, keepdims=True) <= 2 * PART
-        few_last = jnp.sum((row == last).astype(jnp.int32), axis=1, keepdims=True) <= 2 * PART
-        return first, last, few_first, few_last
-
-    def choose(flag, yes, no, out, out_at):
-        @pl.loop(0, PART // SLAB)
+        firsts = jnp.sum((row == first).astype(jnp.int32), axis=1, keepdims=True)
+        lasts = jnp.sum((row == last).astype(jnp.int32), axis=1, keepdims=True)
+        return first, last, firsts, lasts
+
+    def choose(flag, yes, no, out, out_at, size):
+        @pl.loop(0, size // SLAB)
         def _(slab):
             def rows(at):
                 return pl.ds(pl.multiple_of(at + slab * SLAB, SLAB), SLAB)
@@ -168,9 +174,7 @@
         return jnp.transpose(jnp.broadcast_to(row, (128, row.shape[1])))
 
     own = ids_ref[0:1, :]
-    own_first, own_last, own_few_first, own_few_last = ends(own)
-    choose(own_few_last, (u2, PART), (u1, 0), to_r, 0)
-    choose(own_few_first, (u1, PART), (u2, 2 * PART), to_l, PART)
+    own_first, own_last, own_firsts, own_lasts = ends(own)
 
     @pl.loop(0, STEPS - AHEAD)
     def _(step):
@@ -195,30 +199,55 @@
     for copy in ids_out:
         copy.wait()
     l_ids, r_ids, a_ids, d_ids = (ids_in[slot, 0:1, :] for slot in range(4))
-    l_first, l_last, _, l_few_last = ends(l_ids)
-    r_first, r_last, r_few_first, _ = ends(r_ids)
+    l_first, l_last, _, l_lasts = ends(l_ids)
+    r_first, r_last, r_firsts, _ = ends(r_ids)
+    _, a_last, _, a_lasts = ends(a_ids)
+    d_first, _, d_firsts, _ = ends(d_ids)
     whole = own_first == own_last
     relay_r = whole & (l_last == own_first)
     relay_l = whole & (r_first == own_last)
-    l_relays = (l_first == l_last) & (a_ids[:, count - 1:count] == l_first)
-    r_relays = (r_first == r_last) & (d_ids[:, 0:1] == r_last)
+    l_relays = (l_first == l_last) & (a_last == l_first)
+    r_relays = (r_first == r_last) & (d_first == r_last)
+    relay_r_big, relay_r_few = relay_r & (l_lasts > HALF), relay_r & (l_lasts <= HALF)
+    relay_l_big, relay_l_few = relay_l & (r_firsts > HALF), relay_l & (r_firsts <= HALF)
+    l_relays_big, l_relays_few = l_relays & (a_lasts > HALF), l_relays & (a_lasts <= HALF)
+    r_relays_big, r_relays_few = r_relays & (d_firsts > HALF), r_relays & (d_firsts <= HALF)
+    many = 2 * PART
+    own_few_last, own_few_first = own_lasts <= many, own_firsts <= many
+    l_few_last, r_few_first = l_lasts <= many, r_firsts <= many
+    mixed_r, mixed_l = r_relays_big & (own_lasts > many), l_relays_big & (own_firsts > many)
+    l_mixed, r_mixed = relay_l_big & (l_lasts > many), relay_r_big & (r_firsts > many)
+    choose(own_few_last, (u2, PART), (u1, 0), to_r, 0, PART)
+    choose(mixed_r, (u1, HALF), (to_r, 0), to_r, 0, HALF)
+    choose(mixed_r, (u2, PART + HALF), (to_r, HALF), to_r, HALF, HALF)
+    choose(own_few_first, (u1, PART), (u2, 2 * PART), to_l, PART, PART)
+    choose(mixed_l, (u1, PART), (to_l, PART), to_l, PART, HALF)
+    choose(mixed_l, (u2, 2 * PART), (to_l, PART + HALF), to_l, PART + HALF, HALF)
 
     @pl.loop(STEPS - AHEAD, STEPS // 2)
     def _(step):
         right_step(step).wait()
         left_step(step).wait()
 
-    choose(relay_r, (l1, PART), (u2, 2 * PART), to_r, PART)
-    choose(relay_l, (r2, 0), (u1, 0), to_l, 0)
+    choose(relay_r_big, (l1, PART), (u2, 2 * PART), to_r, PART, PART)
+    choose(relay_r_few, (l1, PART + HALF), (to_r, PART), to_r, PART, HALF)
+    choose(relay_l_big, (r2, 0), (u1, 0), to_l, 0, PART)
+    choose(relay_l_few, (r2, 0), (to_l, HALF), to_l, HALF, HALF)
     near_r.start()
     near_l.start()
     l_col[...] = column(l_ids)
     a_col[...] = column(a_ids[:, TOP])
-    mid_ids = jnp.where(l_few_last, l_ids[:, MID], -1)
-    top_ids = jnp.where(l_relays, -1, l_ids[:, TOP])
-    full_l[...] = column(jnp.concatenate([mid_ids, top_ids], axis=1))
-    full_r[0:1, LOW] = jnp.where(r_relays, -2, r_ids[:, LOW])
-    full_r[0:1, MID] = jnp.where(r_few_first, r_ids[:, MID], -2)
+    valid = jnp.concatenate([
+        jnp.where(l_few_last, l_ids[:, 256:384], -1),
+        jnp.where(l_few_last | l_mixed, l_ids[:, 384:512], -1),
+        jnp.where(l_relays, -1, l_ids[:, 512:640]),
+        jnp.where(l_relays_big, -1, l_ids[:, 640:768]),
+    ], axis=1)
+    full_l[...] = column(valid)
+    full_r[0:1, 0:128] = jnp.where(r_relays_big, -2, r_ids[:, 0:128])
+    full_r[0:1, 128:256] = jnp.where(r_relays, -2, r_ids[:, 128:256])
+    full_r[0:1, 256:384] = jnp.where(r_few_first | r_mixed, r_ids[:, 256:384], -2)
+    full_r[0:1, 384:512] = jnp.where(r_few_first, r_ids[:, 384:512], -2)
 
     @pl.loop(STEPS // 2, STEPS)
     def _(step):
@@ -235,19 +264,39 @@
     far_r[1].start()
     far_l[1].start()
 
+    def one_of(flags, blocks):
+        chosen = blocks[-1]
+        for flag, block in zip(flags, blocks[:-1]):
+            chosen = jnp.where(flag, block, chosen)
+        return chosen
+
+    def stacked(top, bottom):
+        return jnp.concatenate([top, bottom], axis=0)
+
+    def beside(first, second):
+        return jnp.concatenate([first, second], axis=1)
+
     sa = dot(l2[MID, :], u1[UPPER, :])
     sa1[...] = sa[:, LOW]
     oo[:, LOW] = dot(l1[...], r1[LOW, :])
     part_l[LOW, :] = s1[MID, TOP]
-    part_l[MID, :] = jnp.where(l_relays, s1[TOP, TOP], s1[MID, LOW])
-    part_l[TOP, :] = jnp.where(l_relays, sa[:, MID], oo[LOW, LOW])
+    part_l[MID, :] = one_of((l_relays_few, l_relays_big, relay_l_big), (
+        stacked(s1[512:640, TOP], sa[0:128, MID]),
+        beside(s1[TOP, 512:640], sa[:, 256:384]),
+        stacked(s1[256:384, LOW], oo[0:128, LOW]),
+        beside(s1[MID, 128:256], oo[LOW, 0:128]),
+    ))
     sums_l.start()
     near_near = dot(l2[MID, :], r2[...])
     sd = dot(u2[LOWER, :], r1[LOW, :])
     sd2[...] = sd[MID, :]
     part_r[LOWER, :] = s2[LOWER, MID]
-    part_r[TOP, :] = jnp.where(relay_r, s2[TOP, MID], s2[LOW, LOW])
-    part_r[FOURTH, :] = jnp.where(relay_r, near_near[:, MID], sd[LOW, :])
+    part_r[TOP, :] = one_of((relay_r_few, relay_r_big, r_relays_big), (
+        stacked(s2[512:640, MID], near_near[128:256, MID]),
+        beside(s2[TOP, 384:512], near_near[:, 384:512]),
+        stacked(s2[128:256, LOW], sd[128:256, :]),
+        beside(s2[LOW, 128:256], sd[LOW, 128:256]),
+    ))
     sums_r.start()
     oo[MID, LOW] = oo[MID, LOW] + near_near[:, LOW]
     oo[MID, MID] = near_near[:, MID]
@@ -271,13 +320,22 @@
         far_l[c].wait()
         above = slice(PART + rows.start, PART + rows.stop)
         beyond = slice(2 * PART + rows.start, 2 * PART + rows.stop)
-        far = dot(l2[rows, :], u1[...])
-        part_l[slice(3 * PART + rows.start, 3 * PART + rows.stop), :] = far[:, TOP]
+        far, far_beside = dot(l2[rows, :], u1[...]), dot(l2[rows, :], r1[LOW, :])
+        if c == 0:
+            first_far, first_beside = far, far_beside
+        else:
+            far = jnp.where(l_mixed, first_far, far)
+            far_beside = jnp.where(l_mixed, first_beside, far_beside)
+        part_l[beyond, :] = far[:, TOP]
         sums_late[c].start()
         s1[rows, :] = far
-        s2[:, beyond] = dot(u2[...], r1[above, :])
-        sd1[rows, :] = dot(l2[rows, :], r1[LOW, :])
-        sa2[:, rows] = dot(l2[MID, :], r1[above, :])
+        sd1[rows, :] = far_beside
+        far, far_beside = dot(u2[...], r1[above, :]), dot(l2[MID, :], r1[above, :])
+        s2[:, beyond] = far
+        sa2[:, rows] = far_beside
+        if c == 1:
+            s2[:, 512:640] = jnp.where(r_mixed, far, s2[:, 512:640])
+            sa2[:, 0:128] = jnp.where(r_mixed, far_beside, sa2[:, 0:128])
         left_found(above, s1[above, :] + dot(l2[rows, :], u2[...]), full_l[rows, 0:1])
         right_found(above, s2[:, above] + dot(u1[...], r1[above, :]), full_r[0:1, above])
         oo[rows, :] = oo[rows, :] + dot(l2[rows, :], r2[...])
@@ -287,51 +345,64 @@
     raised(wide_l, by_row(lifted), UPPER)
     raised(ret_out, by_column(lifted), 1, slice(0, 1), LOWER)
 
-    def either(flag, value, yes, no):
-        raised(yes[0], jnp.where(flag, value, 0.0), *yes[1:])
-        raised(no[0], jnp.where(flag, 0.0, value), *no[1:])
-
     one = slice(0, 1)
+
+    def third(flag, scores, row_ids, col_ids, rows, cols):
+        lifted = lift(scores, row_ids, jnp.where(flag, col_ids, -3))
+        raised(cols[0], by_column(lifted), *cols[1:])
+        raised(rows[0], by_row(lifted), *rows[1:])
+
+    def whole_case(relays, relays_beyond):
+        return jnp.logical_not(relays | relays_beyond)
+
     sums_r.wait()
     lifted = lift(s1[LOWER, MID] + from_l[LOWER, :], l_col[LOWER, 0:1], own[:, MID])
     raised(best, by_column(lifted), one, MID)
     raised(wide_l, by_row(lifted), LOWER)
-    lifted = lift(
-        jnp.where(l_relays, s1[TOP, MID], s1[LOW, LOW]) + from_l[TOP, :],
-        jnp.where(l_relays, l_col[TOP, 0:1], l_col[LOW, 0:1]),
-        jnp.where(l_relays, own[:, MID], own[:, LOW]),
-    )
-    either(l_relays, by_column(lifted), (best, one, MID), (best, one, LOW))
-    either(l_relays, by_row(lifted), (wide_l, TOP), (wide_l, LOW))
-    lifted = lift(
-        jnp.where(l_relays, sa1[...], sd1[...]) + from_l[FOURTH, :],
-        jnp.where(l_relays, a_col[:, 0:1], l_col[LOW, 0:1]),
-        jnp.where(l_relays, own[:, MID], r_ids[:, LOW]),
-    )
-    either(l_relays, by_column(lifted), (best, one, MID), (ret_out, 1, one, LOW))
-    either(l_relays, by_row(lifted), (wide_ll, LOW), (wide_l, LOW))
+    got, a_near = from_l[TOP, :], a_col[:, 0:1]
+    third(l_relays_few, s1[512:640, MID] + got[0:128], l_col[512:640, 0:1], own[:, MID],
+          (wide_l, slice(512, 640)), (best, one, MID))
+    third(l_relays_few, sa1[0:128, :] + got[128:256], a_near[128:256], own[:, MID],
+          (wide_ll, slice(128, 256)), (best, one, MID))
+    third(l_relays_big, s1[TOP, 384:512] + got[:, 0:128], l_col[TOP, 0:1], own[:, 384:512],
+          (wide_l, TOP), (best, one, slice(384, 512)))
+    third(l_relays_big, sa1[:, 128:256] + got[:, 128:256], a_near, own[:, 384:512],
+          (wide_ll, LOW), (best, one, slice(384, 512)))
+    third(relay_l_big, s1[128:256, LOW] + got[0:128], l_col[128:256, 0:1], own[:, LOW],
+          (wide_l, slice(128, 256)), (best, one, LOW))
+    third(relay_l_big, sd1[128:256, :] + got[128:256], l_col[128:256, 0:1], r_ids[:, LOW],
+          (wide_l, slice(128, 256)), (ret_out, 1, one, LOW))
+    rest = whole_case(l_relays, relay_l_big)
+    third(rest, s1[LOW, 128:256] + got[:, 0:128], l_col[LOW, 0:1], own[:, 128:256],
+          (wide_l, LOW), (best, one, slice(128, 256)))
+    third(rest, sd1[:, 0:128] + got[:, 128:256], l_col[LOW, 0:1], r_ids[:, 0:128],
+          (wide_l, LOW), (ret_out, 1, one, slice(0, 128)))
 
     sums_l.wait()
-    lifted = lift(
-        jnp.where(relay_r, s2[TOP, TOP], s2[MID, LOW]) + from_r[MID, :],
-        jnp.where(relay_r, own_col[TOP, 0:1], own_col[MID, 0:1]),
-        jnp.where(relay_r, r_ids[:, TOP], r_ids[:, LOW]),
-    )
-    either(relay_r, by_column(lifted), (ret_out, 1, one, TOP), (ret_out, 1, one, LOW))
-    either(relay_r, by_row(lifted), (wide_own, TOP), (wide_own, MID))
-    lifted = lift(
-        jnp.where(relay_r, sa2[...], sd2[...]) + from_r[TOP, :],
-        jnp.where(relay_r, l_col[TOP, 0:1], own_col[MID, 0:1]),
-        jnp.where(relay_r, r_ids[:, TOP], d_ids[:, LOW]),
-    )
-    either(relay_r, by_column(lifted), (ret_out, 1, one, TOP), (ret_out, 3, one, LOW))
-    either(relay_r, by_row(lifted), (wide_l, TOP), (wide_own, MID))
+    got = from_r[MID, :]
+    third(relay_r_few, s2[512:640, TOP] + got[0:128], own_col[512:640, 0:1], r_ids[:, TOP],
+          (wide_own, slice(512, 640)), (ret_out, 1, one, TOP))
+    third(relay_r_few, sa2[128:256, :] + got[128:256], l_col[640:768, 0:1], r_ids[:, TOP],
+          (wide_l, slice(640, 768)), (ret_out, 1, one, TOP))
+    third(relay_r_big, s2[TOP, 512:640] + got[:, 0:128], own_col[TOP, 0:1], r_ids[:, 512:640],
+          (wide_own, TOP), (ret_out, 1, one, slice(512, 640)))
+    third(relay_r_big, sa2[:, 0:128] + got[:, 128:256], l_col[TOP, 0:1], r_ids[:, 512:640],
+          (wide_l, TOP), (ret_out, 1, one, slice(512, 640)))
+    third(r_relays_big, s2[256:384, LOW] + got[0:128], own_col[256:384, 0:1], r_ids[:, LOW],
+          (wide_own, slice(256, 384)), (ret_out, 1, one, LOW))
+    third(r_relays_big, sd2[0:128, :] + got[128:256], own_col[256:384, 0:1], d_ids[:, LOW],
+          (wide_own, slice(256, 384)), (ret_out, 3, one, LOW))
+    rest = whole_case(relay_r, r_relays_big)
+    third(rest, s2[MID, 128:256] + got[:, 0:128], own_col[MID, 0:1], r_ids[:, 128:256],
+          (wide_own, MID), (ret_out, 1, one, slice(128, 256)))
+    third(rest, sd2[:, 128:256] + got[:, 128:256], own_col[MID, 0:1], d_ids[:, 0:128],
+          (wide_own, MID), (ret_out, 3, one, slice(0, 128)))
     lifted = lift(s2[MID, TOP] + from_r[LOW, :], own_col[MID, 0:1], r_ids[:, TOP])
     raised(ret_out, by_column(lifted), 1, one, TOP)
     raised(wide_own, by_row(lifted), MID)
     for copy in sums_late:
         copy.wait()
-    lifted = lift(s2[LOW, TOP] + from_r[FOURTH, :], own_col[LOW, 0:1], r_ids[:, TOP])
+    lifted = lift(s2[LOW, TOP] + from_r[TOP, :], own_col[LOW, 0:1], r_ids[:, TOP])
     raised(ret_out, by_column(lifted), 1, one, TOP)
     raised(wide_own, by_row(lifted), LOW)
 
@@ -351,7 +422,7 @@
         copy.wait()
     for slot in range(4):
         found = jnp.maximum(found, ret_in[slot, 0:1, :])
-    out_ref[...] = jnp.broadcast_to(found - 1.0, out_ref.shape)
+    out_ref[...] = found - 1.0
 
 
 def solution(mesh):
@@ -359,7 +430,7 @@
 
     def shards(embeddings, cluster_ids):
         count, width = embeddings.shape
-        ids = jnp.broadcast_to(cluster_ids[None, :], (8, count))
+        ids = cluster_ids.reshape(1, count)
         sems = pltpu.SemaphoreType.DMA
 
         def half_rows(rows):
@@ -374,7 +445,7 @@
         slots = STEPS + 1 + PART // LATE
         found = pl.pallas_call(
             lambda *refs: kernel(devices, inner, *refs),
-            out_shape=jax.ShapeDtypeStruct((8, count), jnp.float32),
+            out_shape=jax.ShapeDtypeStruct((1, count), jnp.float32),
             in_specs=[
                 pl.BlockSpec(memory_space=pl.ANY),
                 pl.BlockSpec(memory_space=pltpu.VMEM),
@@ -387,12 +458,11 @@
                 half_rows(2 * PART), half_rows(2 * PART),
                 floats(count, count), floats(count, count), floats(2 * PART, 2 * PART),
                 floats(PART, PART), floats(PART, PART), floats(PART, PART), floats(PART, PART),
-                floats(4 * PART, PART), floats(4 * PART, PART),
-                floats(4 * PART, PART), floats(4 * PART, PART),
-                ints(4, 8, count), ints(count, 128), ints(count, 128), ints(PART, 128),
+                floats(count, PART), floats(count, PART), floats(count, PART), floats(count, PART),
+                ints(4, 1, count), ints(count, 128), ints(count, 128), ints(PART, 128),
                 ints(2 * PART, 128), ints(8, 2 * PART),
                 floats(8, count), floats(count, 128), floats(count, 128), floats(PART, 128),
-                floats(4, 8, count), floats(4, 8, count),
+                floats(4, 1, count), floats(4, 1, count),
                 sems((count // CHUNK,)),
                 sems((slots,)), sems((slots,)), sems((slots,)), sems((slots,)),
                 sems((2 + PART // LATE,)), sems((2 + PART // LATE,)),
@@ -406,7 +476,7 @@
                 transcendentals=count,
             ),
         )(embeddings, ids)
-        return found[0]
+        return found.reshape(count)
 
     return jax.shard_map(
         shards,

time: 134 us -> 126 us (0.940)
  Pallas kernels: 131 us -> 123 us
  local copies, waits for them, and re-layouts: 2.62 us -> 1.27 us
    pallas_call x1, Pallas kernels: 131 us -> 123 us  [shards(): pl.pallas_call(lambda *refs: kernel(devices, inner, *refs), out_shape=jax...]
    slice x1 -> x0, local copies, waits for them, and re-layouts: 1.34 us -> none  [shards(): return found[0]]
where the time goes in v4:
time: 126 us
  Pallas kernels  123 us (98%)
  other arithmetic  1.29 us (1%)
  local copies, waits for them, and re-layouts  1.27 us (1%)
    pallas_call x1, Pallas kernels, shards(): pl.pallas_call(lambda *refs: kernel(devices, inner, *refs), out_shape=jax...  123 us

profile of v4, /device:TPU:0, one launch (start us, length us, event | category | flops | bytes accessed | tf_op | source)
XLA Modules:
  0.0 126.1 jit_solution(4298489404128297947)
XLA Ops:
  0.0 1.3 %reshape.6.refs_1_ = s32[1,768]{1,0:T(1,128)} reshape(s32[768]{0:T(1024)} %param.3) | data formatting | bytes 6144 | tf_op jit(solution)/shard_map/reshape | solution.py:433
  1.3 123.5 %shard_map.28 = f32[1,768]{1,0:T(1,128)} custom-call(bf16[768,4096]{1,0:T(8,128)(2,1)} %refs_0_.1, s32[1,768]{1,0:T(1,128)} %reshape.6.refs_1_), custom_call_target="tpu_custom_call" | custom-call | flops 21743271936 | bytes 6291456 | tf_op jit(solution)/shard_map/pallas_call | solution.py:446
  124.8 1.3 %reduce = f32[768]{0:T(1024)} reduce(f32[1,768]{1,0:T(1,128)} %shard_map.28, f32[]{:T(128)} %constant), dimensions={0}, to_apply=%pallas_call.3.reduce_sub_computation | reduce | bytes 6148 | tf_op jit(solution)/shard_map/pallas_call | solution.py:446

commit v5 on v4

--- a/solution.py
+++ b/solution.py
@@ -44,10 +44,10 @@
 
 def kernel(
     devices, inner,
-    x_ref, ids_ref, out_ref,
-    raw, u1, u2, l1, l2, r1, r2, to_r, to_l, s1, s2, oo, sa1, sd1, sa2, sd2,
-    part_r, part_l, from_l, from_r, ids_in, own_col, l_col, a_col, full_l, full_r,
-    best, wide_own, wide_l, wide_ll, ret_out, ret_in,
+    x_ref, flat_ids, flat_out,
+    raw, u1, u2, l1, l2, r1, r2, to_r, to_l, s1, s2, oo, nn, sdm, sd1, sa2,
+    part_r, part_l, from_l, from_r, ids_ref, ids_in, own_col, l_col, full_l, full_r,
+    best, wide_own, wide_l, ret_out, ret_in,
     raw_sem, send_r, send_l, recv_l, recv_r, part_send, part_recv,
     ids_send, ids_recv, ret_send, ret_recv,
 ):
@@ -60,7 +60,7 @@
         index = lax.rem(me + devices + distance, devices)
         return (index // inner, lax.rem(index, inner))
 
-    prev1, next1, prev2, next2 = device(-1), device(1), device(-2), device(2)
+    prev1, next1 = device(-1), device(1)
 
     def rows_of(chunk):
         return pl.ds(pl.multiple_of(chunk * CHUNK, CHUNK), CHUNK)
@@ -99,27 +99,32 @@
         left_part(STEPS + 1 + c, slice(PART + rows.start, PART + rows.stop))
         for c, rows in enumerate(late)
     ]
-    sums_r = remote(part_r, from_l, part_send.at[0], part_recv.at[0], next1)
+    def sums_right(slot, rows):
+        return remote(
+            part_r.at[rows], from_l.at[rows], part_send.at[slot], part_recv.at[slot], next1
+        )
 
     def sums_left(slot, rows):
         return remote(
             part_l.at[rows], from_r.at[rows], part_send.at[slot], part_recv.at[slot], prev1
         )
 
-    sums_l = sums_left(1, LOWER)
-    sums_late = [
-        sums_left(2 + c, slice(2 * PART + rows.start, 2 * PART + rows.stop))
-        for c, rows in enumerate(late)
+    sums_r = [sums_right(0, slice(384, 640)), sums_right(1, slice(640, 768)), sums_right(5, slice(0, 384))]
+    sums_l = [
+        sums_left(2, slice(256, 384)), sums_left(3, slice(384, 512)),
+        sums_left(4, slice(512, 768)), sums_left(6, slice(0, 256)),
     ]
+
+    barrier = pltpu.get_barrier_semaphore()
+    for target in (prev1, next1):
+        pl.semaphore_signal(barrier, inc=1, device_id=target, device_id_type=MESH)
 
     @pl.loop(0, chunks // 2)
     def _(k):
         load(k).start()
         load(chunks - 1 - k).start()
 
-    barrier = pltpu.get_barrier_semaphore()
-    for target in (prev1, next1, prev2, next2):
-        pl.semaphore_signal(barrier, inc=1, device_id=target, device_id_type=MESH)
+    ids_ref[...] = flat_ids[...].reshape(1, count)
 
     def normalize(chunk):
         load(chunk).wait()
@@ -135,17 +140,21 @@
 
     normalize(0)
     normalize(chunks - 1)
-    pl.semaphore_wait(barrier, 4)
-
-    ids_out = [
-        remote(ids_ref, ids_in.at[slot], ids_send.at[slot], ids_recv.at[slot], target)
-        for slot, target in enumerate((next1, prev1, next2, prev2))
-    ]
+    pl.semaphore_wait(barrier, 2)
+
+    def ids_copy(source, slot, target):
+        return remote(source, ids_in.at[slot], ids_send.at[slot], ids_recv.at[slot], target)
+
+    ids_out = [ids_copy(ids_ref, 0, next1), ids_copy(ids_ref, 1, prev1)]
+    ids_on = [ids_copy(ids_in.at[0], 2, next1), ids_copy(ids_in.at[1], 3, prev1)]
     for copy in ids_out:
         copy.start()
-
     left_step(0).start()
     right_step(0).start()
+    for copy in ids_out:
+        copy.wait()
+    for copy in ids_on:
+        copy.start()
 
     @pl.loop(1, AHEAD)
     def _(k):
@@ -183,7 +192,7 @@
         right_step(step + AHEAD).start()
         left_step(step + AHEAD).start()
 
-    for ref in (best, wide_own, wide_l, wide_ll, ret_out):
+    for ref in (best, wide_own, wide_l, ret_out):
         ref[...] = jnp.zeros_like(ref)
     own_col[...] = column(own)
 
@@ -196,7 +205,7 @@
         lifted = jnp.where(other, lift(scores, own_col[rows, 0:1], own), 0.0)
         raised(best, by_column(lifted), slice(0, 1), slice(0, count))
 
-    for copy in ids_out:
+    for copy in ids_on:
         copy.wait()
     l_ids, r_ids, a_ids, d_ids = (ids_in[slot, 0:1, :] for slot in range(4))
     l_first, l_last, _, l_lasts = ends(l_ids)
@@ -236,7 +245,6 @@
     near_r.start()
     near_l.start()
     l_col[...] = column(l_ids)
-    a_col[...] = column(a_ids[:, TOP])
     valid = jnp.concatenate([
         jnp.where(l_few_last, l_ids[:, 256:384], -1),
         jnp.where(l_few_last | l_mixed, l_ids[:, 384:512], -1),
@@ -277,27 +285,27 @@
         return jnp.concatenate([first, second], axis=1)
 
     sa = dot(l2[MID, :], u1[UPPER, :])
-    sa1[...] = sa[:, LOW]
     oo[:, LOW] = dot(l1[...], r1[LOW, :])
+    sdm[...] = oo[LOW, LOW]
+    near_near = dot(l2[MID, :], r2[...])
+    nn[...] = near_near[:, MID]
+    sd = dot(u2[LOWER, :], r1[LOW, :])
+    l_cases, r_cases = (l_relays_few, l_relays_big, relay_l_big), (relay_r_few, relay_r_big, r_relays_big)
     part_l[LOW, :] = s1[MID, TOP]
-    part_l[MID, :] = one_of((l_relays_few, l_relays_big, relay_l_big), (
-        stacked(s1[512:640, TOP], sa[0:128, MID]),
-        beside(s1[TOP, 512:640], sa[:, 256:384]),
-        stacked(s1[256:384, LOW], oo[0:128, LOW]),
-        beside(s1[MID, 128:256], oo[LOW, 0:128]),
+    part_l[256:384, :] = one_of(l_cases, (
+        sa[0:128, LOW], sa[0:128, 128:384], s1[256:384, LOW],
+        beside(s1[256:384, 128:256], s1[384:512, 128:256]),
     ))
-    sums_l.start()
-    near_near = dot(l2[MID, :], r2[...])
-    sd = dot(u2[LOWER, :], r1[LOW, :])
-    sd2[...] = sd[MID, :]
     part_r[LOWER, :] = s2[LOWER, MID]
-    part_r[TOP, :] = one_of((relay_r_few, relay_r_big, r_relays_big), (
-        stacked(s2[512:640, MID], near_near[128:256, MID]),
-        beside(s2[TOP, 384:512], near_near[:, 384:512]),
-        stacked(s2[128:256, LOW], sd[128:256, :]),
-        beside(s2[LOW, 128:256], sd[LOW, 128:256]),
+    part_r[512:640, :] = one_of(r_cases, (
+        s2[512:640, MID], beside(s2[512:640, 384:512], s2[640:768, 384:512]), sd[128:256, :],
+        beside(sd[0:128, 128:256], sd[128:256, 128:256]),
     ))
-    sums_r.start()
+    sums_l[3].start()
+    sums_r[2].start()
+    part_l[640:768, :] = jnp.where(l_relays_big, sa[128:256, 128:384], sa[0:128, MID])
+    part_r[640:768, :] = jnp.where(r_relays_big, sd[256:384, :],
+                                   beside(sd[256:384, 128:256], sd[384:512, 128:256]))
     oo[MID, LOW] = oo[MID, LOW] + near_near[:, LOW]
     oo[MID, MID] = near_near[:, MID]
     oo[LOW, MID] = jnp.zeros((PART, PART), jnp.float32)
@@ -318,6 +326,9 @@
     for c, rows in enumerate(late):
         far_r[c].wait()
         far_l[c].wait()
+        if c == 1:
+            sums_l[0].start()
+            sums_r[0].start()
         above = slice(PART + rows.start, PART + rows.stop)
         beyond = slice(2 * PART + rows.start, 2 * PART + rows.stop)
         far, far_beside = dot(l2[rows, :], u1[...]), dot(l2[rows, :], r1[LOW, :])
@@ -326,9 +337,14 @@
         else:
             far = jnp.where(l_mixed, first_far, far)
             far_beside = jnp.where(l_mixed, first_beside, far_beside)
-        part_l[beyond, :] = far[:, TOP]
-        sums_late[c].start()
         s1[rows, :] = far
+        part_l[slice(384 + rows.start, 384 + rows.stop), :] = far[:, TOP]
+        if c == 1:
+            part_l[640:768, :] = one_of((l_relays, relay_l_big), (
+                part_l[640:768, :], s1[128:256, LOW],
+                beside(s1[0:128, 128:256], s1[128:256, 128:256]),
+            ))
+        sums_l[1 + c].start()
         sd1[rows, :] = far_beside
         far, far_beside = dot(u2[...], r1[above, :]), dot(l2[MID, :], r1[above, :])
         s2[:, beyond] = far
@@ -336,6 +352,11 @@
         if c == 1:
             s2[:, 512:640] = jnp.where(r_mixed, far, s2[:, 512:640])
             sa2[:, 0:128] = jnp.where(r_mixed, far_beside, sa2[:, 0:128])
+            part_r[640:768, :] = one_of((relay_r_few, relay_r_big), (
+                s2[512:640, TOP], beside(s2[512:640, 512:640], s2[640:768, 512:640]),
+                part_r[640:768, :],
+            ))
+            sums_r[1].start()
         left_found(above, s1[above, :] + dot(l2[rows, :], u2[...]), full_l[rows, 0:1])
         right_found(above, s2[:, above] + dot(u1[...], r1[above, :]), full_r[0:1, above])
         oo[rows, :] = oo[rows, :] + dot(l2[rows, :], r2[...])
@@ -355,74 +376,79 @@
     def whole_case(relays, relays_beyond):
         return jnp.logical_not(relays | relays_beyond)
 
-    sums_r.wait()
+    def halves(block):
+        return stacked(block[:, 0:128], block[:, 128:256])
+
+    sums_r[2].wait()
+    sums_r[0].wait()
     lifted = lift(s1[LOWER, MID] + from_l[LOWER, :], l_col[LOWER, 0:1], own[:, MID])
     raised(best, by_column(lifted), one, MID)
     raised(wide_l, by_row(lifted), LOWER)
-    got, a_near = from_l[TOP, :], a_col[:, 0:1]
-    third(l_relays_few, s1[512:640, MID] + got[0:128], l_col[512:640, 0:1], own[:, MID],
-          (wide_l, slice(512, 640)), (best, one, MID))
-    third(l_relays_few, sa1[0:128, :] + got[128:256], a_near[128:256], own[:, MID],
-          (wide_ll, slice(128, 256)), (best, one, MID))
-    third(l_relays_big, s1[TOP, 384:512] + got[:, 0:128], l_col[TOP, 0:1], own[:, 384:512],
-          (wide_l, TOP), (best, one, slice(384, 512)))
-    third(l_relays_big, sa1[:, 128:256] + got[:, 128:256], a_near, own[:, 384:512],
-          (wide_ll, LOW), (best, one, slice(384, 512)))
-    third(relay_l_big, s1[128:256, LOW] + got[0:128], l_col[128:256, 0:1], own[:, LOW],
-          (wide_l, slice(128, 256)), (best, one, LOW))
-    third(relay_l_big, sd1[128:256, :] + got[128:256], l_col[128:256, 0:1], r_ids[:, LOW],
-          (wide_l, slice(128, 256)), (ret_out, 1, one, LOW))
-    rest = whole_case(l_relays, relay_l_big)
-    third(rest, s1[LOW, 128:256] + got[:, 0:128], l_col[LOW, 0:1], own[:, 128:256],
-          (wide_l, LOW), (best, one, slice(128, 256)))
-    third(rest, sd1[:, 0:128] + got[:, 128:256], l_col[LOW, 0:1], r_ids[:, 0:128],
-          (wide_l, LOW), (ret_out, 1, one, slice(0, 128)))
-
-    sums_l.wait()
-    got = from_r[MID, :]
-    third(relay_r_few, s2[512:640, TOP] + got[0:128], own_col[512:640, 0:1], r_ids[:, TOP],
-          (wide_own, slice(512, 640)), (ret_out, 1, one, TOP))
-    third(relay_r_few, sa2[128:256, :] + got[128:256], l_col[640:768, 0:1], r_ids[:, TOP],
-          (wide_l, slice(640, 768)), (ret_out, 1, one, TOP))
-    third(relay_r_big, s2[TOP, 512:640] + got[:, 0:128], own_col[TOP, 0:1], r_ids[:, 512:640],
-          (wide_own, TOP), (ret_out, 1, one, slice(512, 640)))
-    third(relay_r_big, sa2[:, 0:128] + got[:, 128:256], l_col[TOP, 0:1], r_ids[:, 512:640],
-          (wide_l, TOP), (ret_out, 1, one, slice(512, 640)))
-    third(r_relays_big, s2[256:384, LOW] + got[0:128], own_col[256:384, 0:1], r_ids[:, LOW],
-          (wide_own, slice(256, 384)), (ret_out, 1, one, LOW))
-    third(r_relays_big, sd2[0:128, :] + got[128:256], own_col[256:384, 0:1], d_ids[:, LOW],
-          (wide_own, slice(256, 384)), (ret_out, 3, one, LOW))
-    rest = whole_case(relay_r, r_relays_big)
-    third(rest, s2[MID, 128:256] + got[:, 0:128], own_col[MID, 0:1], r_ids[:, 128:256],
-          (wide_own, MID), (ret_out, 1, one, slice(128, 256)))
-    third(rest, sd2[:, 128:256] + got[:, 128:256], own_col[MID, 0:1], d_ids[:, 0:128],
-          (wide_own, MID), (ret_out, 3, one, slice(0, 128)))
+    sums_l[3].wait()
+    sums_l[0].wait()
     lifted = lift(s2[MID, TOP] + from_r[LOW, :], own_col[MID, 0:1], r_ids[:, TOP])
     raised(ret_out, by_column(lifted), 1, one, TOP)
     raised(wide_own, by_row(lifted), MID)
-    for copy in sums_late:
-        copy.wait()
-    lifted = lift(s2[LOW, TOP] + from_r[TOP, :], own_col[LOW, 0:1], r_ids[:, TOP])
+
+    sums_r[1].wait()
+    early, last = from_l[512:640, :], from_l[640:768, :]
+    near = slice(512, 640)
+    third(l_relays_few, s1[near, MID] + early, l_col[near, 0:1], own[:, MID],
+          (wide_l, near), (best, one, MID))
+    third(l_relays_few, s1[near, TOP] + last, l_col[near, 0:1], own[:, TOP],
+          (wide_l, near), (best, one, TOP))
+    third(l_relays_big, s1[TOP, 384:512] + halves(early), l_col[TOP, 0:1], own[:, 384:512],
+          (wide_l, TOP), (best, one, slice(384, 512)))
+    third(l_relays_big, s1[TOP, 512:640] + halves(last), l_col[TOP, 0:1], own[:, 512:640],
+          (wide_l, TOP), (best, one, slice(512, 640)))
+    third(relay_l_big, sd1[128:256, :] + early, l_col[128:256, 0:1], r_ids[:, LOW],
+          (wide_l, slice(128, 256)), (ret_out, 1, one, LOW))
+    third(relay_l_big, sdm[0:128, :] + last, l_col[256:384, 0:1], r_ids[:, LOW],
+          (wide_l, slice(256, 384)), (ret_out, 1, one, LOW))
+    rest = whole_case(l_relays, relay_l_big)
+    third(rest, sd1[:, 0:128] + halves(early), l_col[LOW, 0:1], r_ids[:, 0:128],
+          (wide_l, LOW), (ret_out, 1, one, slice(0, 128)))
+    third(rest, sdm[:, 0:128] + halves(last), l_col[MID, 0:1], r_ids[:, 0:128],
+          (wide_l, MID), (ret_out, 1, one, slice(0, 128)))
+
+    sums_l[1].wait()
+    sums_l[2].wait()
+    lifted = lift(s2[LOW, TOP] + from_r[384:640, :], own_col[LOW, 0:1], r_ids[:, TOP])
     raised(ret_out, by_column(lifted), 1, one, TOP)
     raised(wide_own, by_row(lifted), LOW)
+    early, last = from_r[256:384, :], from_r[640:768, :]
+    third(relay_r_few, nn[128:256, :] + early, l_col[640:768, 0:1], r_ids[:, MID],
+          (wide_l, slice(640, 768)), (ret_out, 1, one, MID))
+    third(relay_r_few, sa2[128:256, :] + last, l_col[640:768, 0:1], r_ids[:, TOP],
+          (wide_l, slice(640, 768)), (ret_out, 1, one, TOP))
+    third(relay_r_big, beside(nn[:, 128:256], sa2[:, 0:128]) + stacked(early, last),
+          l_col[TOP, 0:1], r_ids[:, 384:640], (wide_l, TOP), (ret_out, 1, one, slice(384, 640)))
+    third(r_relays_big, s2[256:384, LOW] + early, own_col[256:384, 0:1], r_ids[:, LOW],
+          (wide_own, slice(256, 384)), (ret_out, 1, one, LOW))
+    third(r_relays_big, s2[128:256, LOW] + last, own_col[128:256, 0:1], r_ids[:, LOW],
+          (wide_own, slice(128, 256)), (ret_out, 1, one, LOW))
+    rest = whole_case(relay_r, r_relays_big)
+    third(rest, s2[MID, 128:256] + halves(early), own_col[MID, 0:1], r_ids[:, 128:256],
+          (wide_own, MID), (ret_out, 1, one, slice(128, 256)))
+    third(rest, s2[LOW, 128:256] + halves(last), own_col[LOW, 0:1], r_ids[:, 128:256],
+          (wide_own, LOW), (ret_out, 1, one, slice(128, 256)))
 
     def across(wide):
         return by_column(jnp.transpose(wide))
 
     ret_out[0, 0:1, :] = across(wide_l[...])
-    ret_out[2, 0:1, TOP] = across(wide_ll[...])
     back = [
         remote(ret_out.at[slot], ret_in.at[slot], ret_send.at[slot], ret_recv.at[slot], target)
-        for slot, target in enumerate((prev1, next1, prev2, next2))
+        for slot, target in enumerate((prev1, next1))
     ]
     for copy in back:
         copy.start()
     found = jnp.maximum(best[0:1, :], across(wide_own[...]))
     for copy in back:
         copy.wait()
-    for slot in range(4):
+    for slot in range(2):
         found = jnp.maximum(found, ret_in[slot, 0:1, :])
-    out_ref[...] = found - 1.0
+    flat_out[...] = (found - 1.0).reshape(count)
 
 
 def solution(mesh):
@@ -430,7 +456,6 @@
 
     def shards(embeddings, cluster_ids):
         count, width = embeddings.shape
-        ids = cluster_ids.reshape(1, count)
         sems = pltpu.SemaphoreType.DMA
 
         def half_rows(rows):
@@ -445,7 +470,7 @@
         slots = STEPS + 1 + PART // LATE
         found = pl.pallas_call(
             lambda *refs: kernel(devices, inner, *refs),
-            out_shape=jax.ShapeDtypeStruct((1, count), jnp.float32),
+            out_shape=jax.ShapeDtypeStruct((count,), jnp.float32),
             in_specs=[
                 pl.BlockSpec(memory_space=pl.ANY),
                 pl.BlockSpec(memory_space=pltpu.VMEM),
@@ -459,14 +484,14 @@
                 floats(count, count), floats(count, count), floats(2 * PART, 2 * PART),
                 floats(PART, PART), floats(PART, PART), floats(PART, PART), floats(PART, PART),
                 floats(count, PART), floats(count, PART), floats(count, PART), floats(count, PART),
-                ints(4, 1, count), ints(count, 128), ints(count, 128), ints(PART, 128),
+                ints(1, count), ints(4, 1, count), ints(count, 128), ints(count, 128),
                 ints(2 * PART, 128), ints(8, 2 * PART),
-                floats(8, count), floats(count, 128), floats(count, 128), floats(PART, 128),
-                floats(4, 1, count), floats(4, 1, count),
+                floats(8, count), floats(count, 128), floats(count, 128),
+                floats(2, 1, count), floats(2, 1, count),
                 sems((count // CHUNK,)),
                 sems((slots,)), sems((slots,)), sems((slots,)), sems((slots,)),
-                sems((2 + PART // LATE,)), sems((2 + PART // LATE,)),
-                sems((4,)), sems((4,)), sems((4,)), sems((4,)),
+                sems((7,)), sems((7,)),
+                sems((4,)), sems((4,)), sems((2,)), sems((2,)),
             ],
             compiler_params=pltpu.CompilerParams(
                 collective_id=0, has_side_effects=True, vmem_limit_bytes=60 * 1024 * 1024
@@ -475,8 +500,8 @@
                 flops=9 * count * count * width, bytes_accessed=2 * count * width,
                 transcendentals=count,
             ),
-        )(embeddings, ids)
-        return found.reshape(count)
+        )(embeddings, cluster_ids)
+        return found
 
     return jax.shard_map(
         shards,

time: 126 us -> 123 us (0.976)
  Pallas kernels: 123 us -> 121 us
  other arithmetic: 1.29 us -> 0 us
    pallas_call x1, Pallas kernels: 123 us -> 121 us  [shards(): pl.pallas_call(lambda *refs: kernel(devices, inner, *refs), out_shape=jax...]
    pallas_call x1 -> x0, other arithmetic: 1.29 us -> none  [shards(): pl.pallas_call(lambda *refs: kernel(devices, inner, *refs), out_shape=jax...]
    unnamed x0 -> x1, local copies, waits for them, and re-layouts: none -> 1.28 us
    reshape x1 -> x0, local copies, waits for them, and re-layouts: 1.27 us -> none  [shards(): ids = cluster_ids.reshape(1, count)]
where the time goes in v5:
time: 123 us
  Pallas kernels  121 us (98%)
  local copies, waits for them, and re-layouts  1.28 us (1%)
    pallas_call x1, Pallas kernels, shards(): pl.pallas_call(lambda *refs: kernel(devices, inner, *refs), out_shape=jax...  121 us

profile of v5, /device:TPU:0, one launch (start us, length us, event | category | flops | bytes accessed | tf_op | source)
XLA Modules:
  0.0 122.5 jit_solution(14504229348816180719)
XLA Ops:
  0.0 121.3 %shard_map.28 = f32[768]{0:T(1024)} custom-call(bf16[768,4096]{1,0:T(8,128)(2,1)} %refs_0_.1, s32[768]{0:T(1024)} %refs_1_.1), custom_call_target="tpu_custom_call" | custom-call | flops 21743271936 | bytes 6291456 | tf_op jit(solution)/shard_map/pallas_call | solution.py:471
  121.3 1.3 %copy.4 = f32[768]{0:T(1024)} copy(f32[768]{0:T(1024)} %shard_map.28) | data formatting | bytes 6144

commit v6 on v5

--- a/solution.py
+++ b/solution.py
@@ -436,13 +436,13 @@
     def across(wide):
         return by_column(jnp.transpose(wide))
 
-    ret_out[0, 0:1, :] = across(wide_l[...])
     back = [
         remote(ret_out.at[slot], ret_in.at[slot], ret_send.at[slot], ret_recv.at[slot], target)
         for slot, target in enumerate((prev1, next1))
     ]
-    for copy in back:
-        copy.start()
+    back[1].start()
+    ret_out[0, 0:1, :] = across(wide_l[...])
+    back[0].start()
     found = jnp.maximum(best[0:1, :], across(wide_own[...]))
     for copy in back:
         copy.wait()

time: 123 us -> 123 us (level)
  no operation moved by 1% of the time
where the time goes in v6:
time: 123 us; the launch traced here: 122 us
  Pallas kernels  121 us (98%)
  local copies, waits for them, and re-layouts  1.28 us (1%)
    pallas_call x1, Pallas kernels, shards(): pl.pallas_call(lambda *refs: kernel(devices, inner, *refs), out_shape=jax...  121 us

profile of v6, /device:TPU:0, one launch (start us, length us, event | category | flops | bytes accessed | tf_op | source)
XLA Modules:
  0.0 122.5 jit_solution(16901815546074568340)
XLA Ops:
  0.0 121.2 %shard_map.28 = f32[768]{0:T(1024)} custom-call(bf16[768,4096]{1,0:T(8,128)(2,1)} %refs_0_.1, s32[768]{0:T(1024)} %refs_1_.1), custom_call_target="tpu_custom_call" | custom-call | flops 21743271936 | bytes 6291456 | tf_op jit(solution)/shard_map/pallas_call | solution.py:471
  121.2 1.3 %copy.4 = f32[768]{0:T(1024)} copy(f32[768]{0:T(1024)} %shard_map.28) | data formatting | bytes 6144
